TPU v7x, 32 devices: a whole 2x2x4 slice. The times are simulated.
32 devices in a mesh: groups: 2 (over y), space: 4 (over z), tm: 2 (over x), head: 2 (over core).
Axes of the slice: x: 2, y: 2, z: 4, core: 2. Of those that a mesh axis runs over, the one named last changes fastest.
Arguments:
- queries: bfloat16 [12288, 3072], P(('groups', 'space', 'tm'), 'head'), parts along dimension 0, may hold values from -40 to 40
- keys: bfloat16 [12288, 3072], P(('groups', 'space', 'tm'), 'head'), parts along dimension 0, may hold values from -12 to 12
- values: bfloat16 [12288, 3072], P(('groups', 'space', 'tm'), 'head'), parts along dimension 0, may hold values from -6 to 6
- text_keys: bfloat16 [128, 3072], P(('groups', 'space'), 'head'), parts along dimension 0, may hold values from -12 to 12
- text_values: bfloat16 [128, 3072], P(('groups', 'space'), 'head'), parts along dimension 0, may hold values from -6 to 6
- face_dest: int32 [512, 2], P(('groups', 'space', 'tm')), parts along dimension 0, may hold values from 0 to 7, all different within a row; in each aligned block of 32 rows (0 to 31, 32 to 63, ...) at most 16 rows name the same one
Outputs:
- attended: bfloat16 [12288, 3072], P(('groups', 'space', 'tm'), 'head'), parts along dimension 0
There are 2 independent parts, one for each index of `groups`. A program takes and returns all parts, laid end to end along the dimension named above; each array names one. Nothing has to cross between parts.
Inputs may be any that keep to these rules, and one draw needn't show every extreme that they name: `face_dest`: each row names 2 different tile groups. Within the 32 rows of one tile group no tile group is named more than 16 times, and in every draw some tile group is named exactly 16 times there.
All inputs are finite; a program needn't handle non-finite values.
Results may differ from a plain program's by a relative error of at most 0.0029.
Values may be sent and summed in bfloat16 or wider, within the bound.
No kernel may reach another device: no remote copies, remote signals or barrier semaphores. Data moves between devices by JAX's collectives and lax.ppermute only.
A program may use at most 64 MiB of HBM per device.

v0:
```python
import math

import jax
import jax.numpy as jnp
from jax import lax
from jax.sharding import PartitionSpec as P

HD = 128
FACE_ROWS = 4


def face_selection(face_dest, tile_count, slot_count):
    window_blocks, readers = face_dest.shape
    flat_dest = face_dest.reshape(-1)
    owners = jnp.arange(tile_count, dtype=jnp.int32)
    matches = (flat_dest[:, None] == owners[None, :]).astype(jnp.int32)
    earlier = jnp.cumsum(matches, axis=0) - matches
    slot_rank = jnp.sum(earlier * matches, axis=1)
    target = flat_dest * slot_count + slot_rank
    places = jnp.arange(tile_count * slot_count, dtype=jnp.int32)
    chosen = (places[:, None] == target[None, :]).astype(jnp.float32)
    return jnp.sum(chosen.reshape(tile_count * slot_count, window_blocks, readers), axis=2)


def on_device(queries, keys, values, text_keys, text_values, face_dest):
    spaces = lax.axis_size("space")
    frames = lax.axis_size("tm")
    tile_count = spaces * frames
    window_blocks, readers = face_dest.shape
    tok_rows, feature_width = keys.shape
    slot_count = max(2, 2 * window_blocks * readers // tile_count)
    face_span = window_blocks * FACE_ROWS
    slot_rows = slot_count * FACE_ROWS
    chosen = face_selection(face_dest, tile_count, slot_count)
    chosen_bf = chosen.astype(jnp.bfloat16)
    window_face_keys = keys[:face_span].reshape(window_blocks, FACE_ROWS * feature_width)
    window_face_values = values[:face_span].reshape(window_blocks, FACE_ROWS * feature_width)
    send_keys = jnp.dot(chosen_bf, window_face_keys, preferred_element_type=jnp.float32).astype(
        jnp.bfloat16
    )
    send_values = jnp.dot(chosen_bf, window_face_values, preferred_element_type=jnp.float32).astype(
        jnp.bfloat16
    )
    live_slots = jnp.sum(chosen, axis=1).astype(jnp.bfloat16)
    gathered_keys, gathered_values, got_live = (
        lax.all_to_all(
            send_keys.reshape(tile_count, slot_rows, feature_width),
            ("space", "tm"),
            split_axis=0,
            concat_axis=0,
            tiled=True,
        ),
        lax.all_to_all(
            send_values.reshape(tile_count, slot_rows, feature_width),
            ("space", "tm"),
            split_axis=0,
            concat_axis=0,
            tiled=True,
        ),
        lax.all_to_all(
            live_slots.reshape(tile_count, slot_count),
            ("space", "tm"),
            split_axis=0,
            concat_axis=0,
            tiled=True,
        ),
    )
    gathered_keys = gathered_keys.reshape(-1, feature_width)
    gathered_values = gathered_values.reshape(-1, feature_width)
    live_rows = jnp.repeat(got_live.reshape(-1).astype(jnp.float32), FACE_ROWS) > 0.5
    all_text_keys, all_text_values = (
        lax.all_gather(text_keys, "space", axis=0, tiled=True),
        lax.all_gather(text_values, "space", axis=0, tiled=True),
    )
    text_count = all_text_keys.shape[0]
    key_rows = jnp.concatenate([keys, gathered_keys, all_text_keys], axis=0)
    value_rows = jnp.concatenate([values, gathered_values, all_text_values], axis=0)
    key_mask = jnp.concatenate(
        [jnp.ones((tok_rows,), bool), live_rows, jnp.ones((text_count,), bool)]
    )
    head_count = feature_width // HD
    score_scale = 1.0 / math.sqrt(HD)

    def one_head(head_index):
        start = head_index * HD
        query_part = lax.dynamic_slice_in_dim(queries, start, HD, 1)
        key_part = lax.dynamic_slice_in_dim(key_rows, start, HD, 1)
        value_part = lax.dynamic_slice_in_dim(value_rows, start, HD, 1)
        scores = (
            lax.dot_general(
                query_part, key_part, (((1,), (1,)), ((), ())), preferred_element_type=jnp.float32
            )
            * score_scale
        )
        scores = jnp.where(key_mask[None, :], scores, -jnp.inf)
        score_top = jnp.max(scores, axis=1, keepdims=True)
        probs = jnp.exp(scores - score_top)
        totals = jnp.sum(probs, axis=1, keepdims=True)
        mixed = jnp.dot(probs.astype(jnp.bfloat16), value_part, preferred_element_type=jnp.float32)
        return (mixed / totals).astype(jnp.bfloat16)

    per_head = lax.map(one_head, jnp.arange(head_count, dtype=jnp.int32))
    return jnp.transpose(per_head, (1, 0, 2)).reshape(tok_rows, feature_width)


def solution(mesh):
    placed = (
        P(("groups", "space", "tm"), "head"),
        P(("groups", "space", "tm"), "head"),
        P(("groups", "space", "tm"), "head"),
        P(("groups", "space"), "head"),
        P(("groups", "space"), "head"),
        P(("groups", "space", "tm"), None),
    )
    return jax.shard_map(
        on_device,
        mesh=mesh,
        in_specs=placed,
        out_specs=P(("groups", "space", "tm"), "head"),
        check_vma=False,
    )
```

profile of v0, /device:TPU:0, one launch (start us, length us, event | category | flops | bytes accessed | tf_op | source)
XLA Modules:
  0.0 209.7 jit_solution(15050919228824951059)
XLA Ops:
  2.9 7.3 %all-to-all-start = ((bf16[8,1,16]{2,1,0:T(2,128)(2,1)}), bf16[8,1,16]{2,1,0:T(2,128)(2,1)S(1)}, u32[]{:S(2)}, u32[]{:S(2)}) async-start(bf16[8,1,16]{2,1,0:T(2,128)(2,1)} %convert_element_type.48), calls=%async_computation | async-start | bytes 8192 | tf_op jit(solution)/shard_map/all_to_all | solution.py:60
  12.1 2.0 reshape.69
  14.0 2.6 %all-to-all-done = bf16[8,1,16]{2,1,0:T(2,128)(2,1)S(1)} async-done(((bf16[8,1,16]{2,1,0:T(2,128)(2,1)}), bf16[8,1,16]{2,1,0:T(2,128)(2,1)S(1)}, u32[]{:S(2)}, u32[]{:S(2)}) %all-to-all-start) | async-done | bytes 288 | tf_op jit(solution)/shard_map/all_to_all | solution.py:60
  16.6 3.6 %all-to-all-start.1 = ((bf16[8,64,1536]{2,1,0:T(8,128)(2,1)}), bf16[8,64,1536]{2,1,0:T(8,128)(2,1)S(1)}, u32[]{:S(2)}, u32[]{:S(2)}) async-start(bf16[8,64,1536]{2,1,0:T(8,128)(2,1)} %reshape.69), calls=%async_computation.1 | async-start | bytes 3145728 | tf_op jit(solution)/shard_map/all_to_all | solution.py:46
  22.8 2.0 reshape.72
  24.8 31.7 %all-to-all-done.1 = bf16[8,64,1536]{2,1,0:T(8,128)(2,1)S(1)} async-done(((bf16[8,64,1536]{2,1,0:T(8,128)(2,1)}), bf16[8,64,1536]{2,1,0:T(8,128)(2,1)S(1)}, u32[]{:S(2)}, u32[]{:S(2)}) %all-to-all-start.1) | async-done | bytes 1572896 | tf_op jit(solution)/shard_map/all_to_all | solution.py:46
  56.5 3.6 %all-to-all-start.2 = ((bf16[8,64,1536]{2,1,0:T(8,128)(2,1)}), bf16[8,64,1536]{2,1,0:T(8,128)(2,1)S(1)}, u32[]{:S(2)}, u32[]{:S(2)}) async-start(bf16[8,64,1536]{2,1,0:T(8,128)(2,1)} %reshape.72), calls=%async_computation.2 | async-start | bytes 3145728 | tf_op jit(solution)/shard_map/all_to_all | solution.py:53
  60.1 44.9 %all_gather.6 = bf16[64,1536]{1,0:T(8,128)(2,1)S(1)} all-gather(bf16[16,1536]{1,0:T(8,128)(2,1)S(1)} %copy-done), channel_id=1, replica_groups=mesh['groups'=2,'space'=4,'tm'=2,'head'=2] {'space'}, dimensions={0}, use_global_device_ids=true | all-gather | bytes 245760 | tf_op jit(solution)/shard_map/all_gather | solution.py:72
  105.0 13.8 %all_gather.7 = bf16[64,1536]{1,0:T(8,128)(2,1)S(1)} all-gather(bf16[16,1536]{1,0:T(8,128)(2,1)} %param.12), channel_id=1, replica_groups=mesh['groups'=2,'space'=4,'tm'=2,'head'=2] {'space'}, dimensions={0}, use_global_device_ids=true | all-gather | bytes 245760 | tf_op jit(solution)/shard_map/all_gather | solution.py:73
  121.4 3.4 %pad_maximum_fusion = bf16[1344,1536]{1,0:T(8,128)(2,1)} fusion(bf16[64,1536]{1,0:T(8,128)(2,1)S(1)} %all_gather.6, bf16[512,1536]{1,0:T(8,128)(2,1)S(1)} %bitcast.16, bf16[768,1536]{1,0:T(8,128)(2,1)} %param.9), kind=kLoop, calls=%fused_computation.17 | loop fusion | flops 12386304 | bytes 8257536 | tf_op jit(solution)/shard_map/concatenate | solution.py:76
  124.8 3.4 %pad_maximum_fusion.1 = bf16[1344,1536]{1,0:T(8,128)(2,1)} fusion(bf16[64,1536]{1,0:T(8,128)(2,1)S(1)} %all_gather.7, bf16[512,1536]{1,0:T(8,128)(2,1)S(1)} %bitcast.17, bf16[768,1536]{1,0:T(8,128)(2,1)} %param.10), kind=kLoop, calls=%fused_computation.18 | loop fusion | flops 12386304 | bytes 8257536 | tf_op jit(solution)/shard_map/concatenate | solution.py:77
  128.2 77.2 %while.10 = (s32[]{:T(128)}, bf16[12,768,128]{1,2,0:T(8,128)(2,1)}, pred[1344]{0:T(1024)(128)(4,1)S(1)}, s32[12]{0:T(128)S(1)}, bf16[768,1536]{1,0:T(8,128)(2,1)...) while((s32[]{:T(128)}, bf16[12,768,128]{1,2,0:T(8,128)(2,1)}, ...), condition=%wide.region_7.8_spmd, body=%wide.region_4.7_spmd.sunk | while | flops 535902720 | bytes 14272491 | solution.py:102
  129.6 1.8 fusion.34
  132.0 1.8 fusion.36
  136.1 1.8 fusion.34
  138.5 1.8 fusion.36
  142.5 1.8 fusion.34
  148.9 1.8 fusion.34
  151.3 1.8 fusion.36
  155.4 1.8 fusion.34
  157.8 1.8 fusion.36
  161.8 1.8 fusion.34
  168.2 1.8 fusion.34
  170.7 1.8 fusion.36
  174.7 1.8 fusion.34
  181.1 1.8 fusion.34
  183.5 1.8 fusion.36
  187.5 1.8 fusion.34
  189.9 1.8 fusion.36
  193.9 1.8 fusion.34
  200.4 1.8 fusion.34
  205.4 4.3 %copy.39 = bf16[768,1536]{1,0:T(8,128)(2,1)} copy(bf16[768,1536]{0,1:T(8,128)(2,1)} %bitcast.18) | data formatting | bytes 4718592 | tf_op jit(solution)/shard_map/reshape | solution.py:103
  (82 shorter events, 44.3 us)
Async XLA Ops:
  2.9 13.7 %all-to-all-start = ((bf16[8,1,16]{2,1,0:T(2,128)(2,1)}), bf16[8,1,16]{2,1,0:T(2,128)(2,1)S(1)}, u32[]{:S(2)}, u32[]{:S(2)}) async-start(bf16[8,1,16]{2,1,0:T(2,128)(2,1)} %convert_element_type.48), calls=%async_computation | async-start | bytes 8192 | tf_op jit(solution)/shard_map/all_to_all | solution.py:60
  11.4 8.8 %slice-start = ((bf16[768,1536]{1,0:T(8,128)(2,1)}), bf16[128,1536]{1,0:T(8,128)(2,1)S(1)}, s32[]{:S(2)}) async-start(bf16[768,1536]{1,0:T(8,128)(2,1)} %param.10), calls=%async_computation.3 | async-start | bytes 786432 | tf_op jit(solution)/shard_map/slice | solution.py:37
  16.6 39.8 %all-to-all-start.1 = ((bf16[8,64,1536]{2,1,0:T(8,128)(2,1)}), bf16[8,64,1536]{2,1,0:T(8,128)(2,1)S(1)}, u32[]{:S(2)}, u32[]{:S(2)}) async-start(bf16[8,64,1536]{2,1,0:T(8,128)(2,1)} %reshape.69), calls=%async_computation.1 | async-start | bytes 3145728 | tf_op jit(solution)/shard_map/all_to_all | solution.py:46
  21.2 38.9 %copy-start = (bf16[16,1536]{1,0:T(8,128)(2,1)S(1)}, bf16[16,1536]{1,0:T(8,128)(2,1)}, u32[]{:S(2)}) copy-start(bf16[16,1536]{1,0:T(8,128)(2,1)} %param.11) | copy-start | bytes 147460
  56.5 68.4 %all-to-all-start.2 = ((bf16[8,64,1536]{2,1,0:T(8,128)(2,1)}), bf16[8,64,1536]{2,1,0:T(8,128)(2,1)S(1)}, u32[]{:S(2)}, u32[]{:S(2)}) async-start(bf16[8,64,1536]{2,1,0:T(8,128)(2,1)} %reshape.72), calls=%async_computation.2 | async-start | bytes 3145728 | tf_op jit(solution)/shard_map/all_to_all | solution.py:53
where the time goes:
time: 211 us; the launch traced here: 210 us
  blocking collectives  58.7 us (28%)
  matrix products  45.3 us (21%)
  waiting for transfers between devices  34.3 us (16%)
  local copies, waits for them, and re-layouts  32.3 us (15%)
  other arithmetic  16 us (8%)
  starting transfers between devices  14.5 us (7%)
  loops' own time  8.62 us (4%)
    all_gather x1, blocking collectives, on_device(): lax.all_gather(text_keys, 'space', axis=0, tiled=True)  44.9 us
    all_to_all x1, waiting for transfers between devices, on_device(): lax.all_to_all(send_keys.reshape(tile_count, slot_rows, feature_width), (...  31.7 us
    dot_general x12, matrix products, one_head(): lax.dot_general(query_part, key_part, (((1,), (1,)), ((), ())), preferred...  21.7 us
    dot_general x12, matrix products, one_head(): jnp.dot(probs.astype(jnp.bfloat16), value_part, preferred_element_type=jn...  21.4 us
    all_gather x1, blocking collectives, on_device(): lax.all_gather(text_values, 'space', axis=0, tiled=True)  13.8 us
    dynamic_update_slice x24, local copies, waits for them, and re-layouts, on_device(): per_head = lax.map(one_head, jnp.arange(head_count, dtype=jnp.int32))  10.2 us
    another operation x1, loops' own time, on_device(): per_head = lax.map(one_head, jnp.arange(head_count, dtype=jnp.int32))  8.62 us
    dynamic_slice x12, local copies, waits for them, and re-layouts, on_device(): per_head = lax.map(one_head, jnp.arange(head_count, dtype=jnp.int32))  7.94 us
  transfers between devices with their start and end apart: 3, of which 2 were waited for; matrix products, arithmetic and copies ran while one was open for 7% of the time, Pallas kernels for 0%

commit v1 on v0

v1 whole, which is shorter than its diff:
```python
import functools
import math

import jax
import jax.numpy as jnp
from jax import lax
from jax.experimental import pallas as pl
from jax.experimental.pallas import tpu as pltpu
from jax.sharding import PartitionSpec as P

HD = 128
FACE_ROWS = 4
GROUPS = 3
TILE_Q = 256
LOG2E = 1.4426950408889634
BF = jnp.bfloat16
F32 = jnp.float32


def face_selection(face_dest, tile_count, slot_count):
    window_blocks, readers = face_dest.shape
    flat_dest = face_dest.reshape(-1)
    owners = jnp.arange(tile_count, dtype=jnp.int32)
    matches = (flat_dest[:, None] == owners[None, :]).astype(jnp.int32)
    earlier = jnp.cumsum(matches, axis=0) - matches
    slot_rank = jnp.sum(earlier * matches, axis=1)
    target = flat_dest * slot_count + slot_rank
    places = jnp.arange(tile_count * slot_count, dtype=jnp.int32)
    chosen = (places[:, None] == target[None, :]).astype(jnp.float32)
    return jnp.sum(chosen.reshape(tile_count * slot_count, window_blocks, readers), axis=2)


def attention_kernel(has_out, part_count, *refs):
    q_ref, k_ref, v_ref, text_k_ref, text_v_ref, live_ref = refs[:6]
    part_refs = refs[6 : 6 + part_count]
    out_ref, key_rows, value_rows = refs[6 + part_count + has_out :]
    tok_rows = k_ref.shape[0]
    text_rows = text_k_ref.shape[0]
    received = live_ref.shape[0]
    scale = LOG2E / math.sqrt(HD)
    key_rows[0:tok_rows, :] = k_ref[...]
    value_rows[0:tok_rows, 0:HD] = v_ref[...]
    value_rows[0:tok_rows, HD:] = jnp.ones((tok_rows, HD), BF)
    at = tok_rows
    spare = k_ref[0:1, :]
    for part in part_refs:
        half = part.shape[0] // 2
        flags = live_ref[at - tok_rows : at - tok_rows + half, :]
        key_rows[at : at + half, :] = jnp.where(flags > 0, part[0:half, :], spare)
        value_rows[at : at + half, 0:HD] = part[half:, :]
        value_rows[at : at + half, HD:] = flags
        at += half
    key_rows[at:, :] = text_k_ref[...]
    value_rows[at:, 0:HD] = text_v_ref[...]
    value_rows[at:, HD:] = jnp.ones((text_rows, HD), BF)
    for start in range(0, q_ref.shape[0], TILE_Q):
        scores = lax.dot_general(
            q_ref[start : start + TILE_Q, :],
            key_rows[...],
            (((1,), (1,)), ((), ())),
            preferred_element_type=F32,
        )
        top = jnp.max(scores, axis=1, keepdims=True)
        weights = jnp.exp2((scores - top) * scale).astype(BF)
        mixed = jnp.dot(weights, value_rows[...], preferred_element_type=F32)
        out_ref[start : start + TILE_Q, :] = (mixed[:, :HD] / mixed[:, HD:]).astype(BF)


def attention(group, heads, queries, keys, values, text_k, text_v, live, parts, out):
    tok_rows, width = queries.shape
    text_rows = text_k.shape[0]
    received = live.shape[0]
    total = tok_rows + received + text_rows
    first = group * heads
    col = lambda h: (0, first + h)
    here = lambda h: (0, h)
    specs = [
        pl.BlockSpec((tok_rows, HD), col),
        pl.BlockSpec((tok_rows, HD), col),
        pl.BlockSpec((tok_rows, HD), col),
        pl.BlockSpec((text_rows, HD), col),
        pl.BlockSpec((text_rows, HD), col),
        pl.BlockSpec((received, HD), lambda h: (0, 0)),
    ]
    operands = [queries, keys, values, text_k, text_v, live]
    for part in parts:
        specs.append(pl.BlockSpec((part.shape[0], HD), here))
        operands.append(part)
    aliases = {}
    if out is not None:
        aliases = {len(operands): 0}
        specs.append(pl.BlockSpec(memory_space=pl.ANY))
        operands.append(out)
    return pl.pallas_call(
        functools.partial(attention_kernel, int(out is not None), len(parts)),
        grid=(heads,),
        out_shape=jax.ShapeDtypeStruct((tok_rows, width), BF),
        in_specs=specs,
        out_specs=pl.BlockSpec((tok_rows, HD), col),
        scratch_shapes=[pltpu.VMEM((total, HD), BF), pltpu.VMEM((total, 2 * HD), BF)],
        input_output_aliases=aliases,
        compiler_params=pltpu.CompilerParams(vmem_limit_bytes=40 * 1024 * 1024),
        cost_estimate=pl.CostEstimate(
            flops=heads * 6 * HD * tok_rows * total,
            bytes_accessed=heads * HD * 2 * (4 * tok_rows + 2 * received),
            transcendentals=heads * tok_rows * total,
        ),
        name="attention%d" % group,
    )(*operands)


def places_kernel(slot_rows, hits_ref, choose_ref, live_ref):
    span = hits_ref.shape[1]
    sources = 4
    hits = hits_ref[...]
    row = lax.broadcasted_iota(jnp.int32, (span, span), 0)
    column = lax.broadcasted_iota(jnp.int32, (span, span), 1)
    before = (row < column) & (row % FACE_ROWS == column % FACE_ROWS)
    rank = jnp.dot(hits.astype(BF), before.astype(BF), preferred_element_type=F32)
    member = (lax.broadcasted_iota(jnp.int32, hits.shape, 1) % FACE_ROWS).astype(F32)
    target = jnp.where(hits > 0, rank * FACE_ROWS + member, -1.0)
    slot = lax.broadcasted_iota(jnp.int32, (slot_rows, span), 0).astype(F32)
    ones = jnp.ones((span, HD), BF)
    for source in range(sources):
        mine = (slot == target[source : source + 1, :]).astype(F32).astype(BF)
        sent = (slot == target[sources + source : sources + source + 1, :]).astype(F32).astype(BF)
        come = (slot == target[2 * sources + source : 2 * sources + source + 1, :]).astype(F32).astype(BF)
        base = source * slot_rows
        choose_ref[2 * base : 2 * base + slot_rows, :] = mine
        choose_ref[2 * base + slot_rows : 2 * base + 2 * slot_rows, :] = sent
        live_ref[base : base + slot_rows, :] = jnp.dot(mine, ones, preferred_element_type=F32).astype(BF)
        base += sources * slot_rows
        live_ref[base : base + slot_rows, :] = jnp.dot(come, ones, preferred_element_type=F32).astype(BF)


def pick_kernel(slot_rows, choose_ref, own_ref, pair_ref, pa_ref, pb_ref, qa_ref, qb_ref, mine_ref, sent_ref):
    half = own_ref.shape[0] // 2
    block = 4 * slot_rows
    for source in range(4):
        choose = choose_ref[2 * slot_rows * source : 2 * slot_rows * (source + 1), :]
        for part in range(2):
            rows = slice(part * half, (part + 1) * half)
            if source == 0:
                held = own_ref[rows, :]
            elif source == 1:
                held = pair_ref[rows, :]
            elif source == 2:
                held = pa_ref[rows, :] + qa_ref[rows, :]
            else:
                held = pb_ref[rows, :] + qb_ref[rows, :]
            got = jnp.dot(choose, held, preferred_element_type=F32).astype(BF)
            base = part * block + source * slot_rows
            mine_ref[base : base + slot_rows, :] = got[:slot_rows, :]
            sent_ref[base : base + slot_rows, :] = got[slot_rows:, :]


def pick(group, slot_rows, choose, arrays):
    span2, width = arrays[0].shape
    whole = lambda a: pl.BlockSpec(a.shape, lambda: (0, 0))
    shape = jax.ShapeDtypeStruct((8 * slot_rows, width), BF)
    spec = pl.BlockSpec(shape.shape, lambda: (0, 0))
    return pl.pallas_call(
        functools.partial(pick_kernel, slot_rows),
        out_shape=(shape, shape),
        in_specs=[whole(a) for a in (choose, *arrays)],
        out_specs=(spec, spec),
        compiler_params=pltpu.CompilerParams(vmem_limit_bytes=24 * 1024 * 1024),
        cost_estimate=pl.CostEstimate(
            flops=4 * 2 * 2 * 2 * slot_rows * span2 // 2 * width,
            bytes_accessed=8 * span2 * width * 2,
            transcendentals=0,
        ),
        name="pick%d" % group,
    )(choose, *arrays)


def chained(queries, keys, values, text_keys, text_values, face_dest):
    spaces = lax.axis_size("space")
    frames = lax.axis_size("tm")
    tile_count = spaces * frames
    window_blocks, readers = face_dest.shape
    tok_rows, width = keys.shape
    slot_count = max(2, 2 * window_blocks * readers // tile_count)
    span = window_blocks * FACE_ROWS
    slot_rows = slot_count * FACE_ROWS
    z = lax.axis_index("space")
    x = lax.axis_index("tm")
    head_count = width // HD
    heads = head_count // GROUPS
    cols = heads * HD

    ends = [(0, 1), (1, 0), (2, 3), (3, 2)]
    inner = [(1, 2), (2, 1)]
    outward = [(1, 0), (2, 3)]
    own = [
        jnp.concatenate(
            [keys[:span, g * cols : (g + 1) * cols], values[:span, g * cols : (g + 1) * cols]], axis=0
        )
        for g in range(GROUPS)
    ]
    all_dest = lax.all_gather(face_dest, ("space", "tm"), axis=0, tiled=False)
    text = lax.all_gather(jnp.stack([text_keys, text_values]), "space", axis=1, tiled=True)
    all_dest = all_dest.reshape(spaces, frames, window_blocks, readers)
    order = jnp.where(z < 2, jnp.array([0, 1, 2, 3]), jnp.array([3, 2, 1, 0]))
    swap = (z == 1) | (z == 2)
    order = jnp.where(swap, jnp.stack([order[1], order[0], order[2], order[3]]), order)
    dest = all_dest[order]
    mine_line = lax.dynamic_index_in_dim(dest, x, 1, keepdims=False)
    other_line = lax.dynamic_index_in_dim(dest, 1 - x, 1, keepdims=False)
    me = z * frames + x
    partner = z * frames + 1 - x
    hits = jnp.stack(
        [
            jnp.any(mine_line == me, axis=2),
            jnp.any(mine_line == partner, axis=2),
            jnp.any(other_line == me, axis=2),
            jnp.zeros((spaces, window_blocks), bool),
        ]
    ).astype(F32)
    hits = jnp.repeat(hits.reshape(4 * spaces, window_blocks), FACE_ROWS, axis=1)
    choose, live = pl.pallas_call(
        functools.partial(places_kernel, slot_rows),
        out_shape=(
            jax.ShapeDtypeStruct((8 * slot_rows, span), BF),
            jax.ShapeDtypeStruct((8 * slot_rows, HD), BF),
        ),
        name="places",
    )(hits)

    pair = [lax.ppermute(a, "space", ends) for a in own]
    pa = [lax.ppermute(a, "space", inner) for a in own]
    pb = [lax.ppermute(a, "space", inner) for a in pair]
    qa = [lax.ppermute(a, "space", outward) for a in pa]
    qb = [lax.ppermute(a, "space", outward) for a in pb]
    out = None
    for g in range(GROUPS):
        mine, sent = pick(g, slot_rows, choose, (own[g], pair[g], pa[g], pb[g], qa[g], qb[g]))
        came = lax.ppermute(sent, "tm", [(0, 1), (1, 0)])
        out = attention(g, heads, queries, keys, values, text[0], text[1], live, (mine, came), out)
    return out


def exchanged(queries, keys, values, text_keys, text_values, face_dest):
    spaces = lax.axis_size("space")
    frames = lax.axis_size("tm")
    tile_count = spaces * frames
    window_blocks, readers = face_dest.shape
    tok_rows, width = keys.shape
    slot_count = max(2, 2 * window_blocks * readers // tile_count)
    span = window_blocks * FACE_ROWS
    slot_rows = slot_count * FACE_ROWS
    chosen = face_selection(face_dest, tile_count, slot_count)

    def exchange(rows):
        blocks = rows[:span].reshape(window_blocks, FACE_ROWS * width)
        send = jnp.dot(chosen.astype(BF), blocks, preferred_element_type=F32).astype(BF)
        send = send.reshape(tile_count, slot_rows, width)
        got = lax.all_to_all(send, ("space", "tm"), split_axis=0, concat_axis=0, tiled=True)
        return got.reshape(-1, width)

    live_slots = jnp.sum(chosen, axis=1).astype(BF).reshape(tile_count, slot_count)
    got_live = lax.all_to_all(live_slots, ("space", "tm"), split_axis=0, concat_axis=0, tiled=True)
    live = jnp.repeat(got_live.reshape(-1, 1), FACE_ROWS, axis=0)
    live = jnp.broadcast_to(live, (live.shape[0], HD))
    received = jnp.concatenate([exchange(keys), exchange(values)], axis=0)
    text_k = lax.all_gather(text_keys, "space", axis=0, tiled=True)
    text_v = lax.all_gather(text_values, "space", axis=0, tiled=True)
    return attention(0, width // HD, queries, keys, values, text_k, text_v, live, (received,), None)


def on_device(*arrays):
    if lax.axis_size("space") == 4 and lax.axis_size("tm") == 2:
        return chained(*arrays)
    return exchanged(*arrays)


def solution(mesh):
    placed = (
        P(("groups", "space", "tm"), "head"),
        P(("groups", "space", "tm"), "head"),
        P(("groups", "space", "tm"), "head"),
        P(("groups", "space"), "head"),
        P(("groups", "space"), "head"),
        P(("groups", "space", "tm"), None),
    )
    return jax.shard_map(
        on_device,
        mesh=mesh,
        in_specs=placed,
        out_specs=P(("groups", "space", "tm"), "head"),
        check_vma=False,
    )
```

time: 211 us -> 124 us (0.59)
  matrix products: 45.3 us -> 0 us
  Pallas kernels: 0 us -> 36.1 us
  waiting for transfers between devices: 34.3 us -> 7.2 us
  local copies, waits for them, and re-layouts: 32.3 us -> 6.69 us
  blocking collectives: 58.7 us -> 43.7 us
  other arithmetic: 16 us -> 1.55 us
  starting transfers between devices: 14.5 us -> 27.5 us
  loops' own time: 8.62 us -> 0 us
    dot_general x26 -> x0, matrix products: 45.3 us -> none  [the longest x12 21.7 us: one_head(): lax.dot_general(query_part, key_part, (((1,), (1,)), ((), ())), preferred...]
    pallas_call x0 -> x7, Pallas kernels: none -> 36.1 us  [the longest x3 29.5 us: attention(): pl.pallas_call(functools.partial(attention_kernel, int(out is not None),...]
    all_to_all x3 -> x0, waiting for transfers between devices: 34.3 us -> none  [the longest x1 31.7 us: on_device(): lax.all_to_all(send_keys.reshape(tile_count, slot_rows, feature_width), (...]
    ppermute x0 -> x18, starting transfers between devices: none -> 27.5 us  [the longest x3 7.54 us: chained(): pair = [lax.ppermute(a, 'space', ends) for a in own]]
    all_gather x2, blocking collectives: 58.7 us -> 43.7 us  [the longest x1 25.5 us: chained(): all_dest = lax.all_gather(face_dest, ('space', 'tm'), axis=0, tiled=False)]
    all_to_all x3 -> x0, starting transfers between devices: 14.5 us -> none  [the longest x1 7.25 us: on_device(): lax.all_to_all(live_slots.reshape(tile_count, slot_count), ('space', 'tm'...]
    dynamic_update_slice x24 -> x0, local copies, waits for them, and re-layouts: 10.2 us -> none  [on_device(): per_head = lax.map(one_head, jnp.arange(head_count, dtype=jnp.int32))]
    another operation x1 -> x0, loops' own time: 8.62 us -> none  [on_device(): per_head = lax.map(one_head, jnp.arange(head_count, dtype=jnp.int32))]
  transfers between devices with their start and end apart: 3 -> 18, of which waited for: 2 -> 3; matrix products, arithmetic and copies ran while one was open for 7% -> 4% of each run, Pallas kernels for 0% -> 21%
where the time goes in v1:
time: 124 us; the launch traced here: 123 us
  blocking collectives  43.7 us (35%)
  Pallas kernels  36.1 us (29%)
  starting transfers between devices  27.5 us (22%)
  waiting for transfers between devices  7.2 us (6%)
  local copies, waits for them, and re-layouts  6.69 us (5%)
  other arithmetic  1.55 us (1%)
    pallas_call x3, Pallas kernels, attention(): pl.pallas_call(functools.partial(attention_kernel, int(out is not None),...  29.5 us
    all_gather x1, blocking collectives, chained(): all_dest = lax.all_gather(face_dest, ('space', 'tm'), axis=0, tiled=False)  25.5 us
    all_gather x1, blocking collectives, chained(): lax.all_gather(jnp.stack([text_keys, text_values]), 'space', axis=1, tile...  18.1 us
    ppermute x3, starting transfers between devices, chained(): pair = [lax.ppermute(a, 'space', ends) for a in own]  7.54 us
    pallas_call x3, Pallas kernels, pick(): pl.pallas_call(functools.partial(pick_kernel, slot_rows), out_shape=(shap...  4.96 us
    ppermute x3, starting transfers between devices, chained(): pb = [lax.ppermute(a, 'space', inner) for a in pair]  4.26 us
    ppermute x3, starting transfers between devices, chained(): pa = [lax.ppermute(a, 'space', inner) for a in own]  4.08 us
    ppermute x3, starting transfers between devices, chained(): came = lax.ppermute(sent, 'tm', [(0, 1), (1, 0)])  3.95 us
  transfers between devices with their start and end apart: 18, of which 3 were waited for; matrix products, arithmetic and copies ran while one was open for 4% of the time, Pallas kernels for 21%

profile of v1, /device:TPU:0, one launch (start us, length us, event | category | flops | bytes accessed | tf_op | source)
XLA Modules:
  0.0 123.0 jit_solution(1374501554953300933)
XLA Ops:
  0.0 1.3 %fusion = (bf16[128,512]{1,0:T(8,128)(2,1)S(1)}, bf16[128,512]{1,0:T(8,128)(2,1)S(1)}, bf16[128,512]{1,0:T(8,128)(2,1)S(1)}, bf16[128,512]{1,0:T(8,128)(2,1)S(1)...) fusion(bf16[768,1536]{1,0:T(8,128)(2,1)} %refs_1_.5, bf16[768,1536]{1,0:T(8,128)(2,1)} %refs_2_.5), kind=kLoop, calls=%fused_computation.15 | loop fusion | bytes 1572864 | tf_op jit(solution)/shard_map/slice | solution.py:197
  1.3 3.1 %collective-permute-start.12 = (bf16[256,512]{1,0:T(8,128)(2,1)S(1)}, bf16[256,512]{1,0:T(8,128)(2,1)}, u32[]{:S(2)}, u32[]{:S(2)}) collective-permute-start(bf16[256,512]{1,0:T(8,128)(2,1)S(1)} %pad_maximum_fusion.2.own_ref), channel_id=1, source_target_pairs={{0,4},{4,0},{8,12},{12,8},{1,5},{5,1},{9,13},{13,9},{2,6},{6,2},{1... | collective-permute-start | bytes 786440 | tf_op jit(solution)/shard_map/ppermute | solution.py:230
  4.5 1.4 %collective-permute-start.13 = (bf16[256,512]{1,0:T(8,128)(2,1)S(1)}, bf16[256,512]{1,0:T(8,128)(2,1)}, u32[]{:S(2)}, u32[]{:S(2)}) collective-permute-start(bf16[256,512]{1,0:T(8,128)(2,1)S(1)} %pad_maximum_fusion.2.own_ref), channel_id=1, source_target_pairs={{4,8},{8,4},{5,9},{9,5},{6,10},{10,6},{7,11},{11,7},{20,24},{24,20... | collective-permute-start | bytes 786440 | tf_op jit(solution)/shard_map/ppermute | solution.py:231
  5.8 3.8 %collective-permute-start.6 = (bf16[256,512]{1,0:T(8,128)(2,1)S(1)}, bf16[256,512]{1,0:T(8,128)(2,1)}, u32[]{:S(2)}, u32[]{:S(2)}) collective-permute-start(bf16[256,512]{1,0:T(8,128)(2,1)S(1)} %pad_maximum_fusion.1.own_ref), channel_id=1, source_target_pairs={{0,4},{4,0},{8,12},{12,8},{1,5},{5,1},{9,13},{13,9},{2,6},{6,2},{1... | collective-permute-start | bytes 786440 | tf_op jit(solution)/shard_map/ppermute | solution.py:230
  9.6 1.3 %collective-permute-start.7 = (bf16[256,512]{1,0:T(8,128)(2,1)S(1)}, bf16[256,512]{1,0:T(8,128)(2,1)}, u32[]{:S(2)}, u32[]{:S(2)}) collective-permute-start(bf16[256,512]{1,0:T(8,128)(2,1)S(1)} %pad_maximum_fusion.1.own_ref), channel_id=1, source_target_pairs={{4,8},{8,4},{5,9},{9,5},{6,10},{10,6},{7,11},{11,7},{20,24},{24,20... | collective-permute-start | bytes 786440 | tf_op jit(solution)/shard_map/ppermute | solution.py:231
  11.7 1.5 %collective-permute-start.14 = (bf16[256,512]{1,0:T(8,128)(2,1)}, bf16[256,512]{1,0:T(8,128)(2,1)}, u32[]{:S(2)}, u32[]{:S(2)}) collective-permute-start(bf16[256,512]{1,0:T(8,128)(2,1)} %collective-permute-done.12.pair_ref), channel_id=1, source_target_pairs={{4,8},{8,4},{5,9},{9,5},{6,10},{10,6},{7,11},{11,7},{20,24},{24,20... | collective-permute-start | bytes 786440 | tf_op jit(solution)/shard_map/ppermute | solution.py:232
  13.9 1.3 %collective-permute-start.15 = (bf16[256,512]{1,0:T(8,128)(2,1)}, bf16[256,512]{1,0:T(8,128)(2,1)}, u32[]{:S(2)}, u32[]{:S(2)}) collective-permute-start(bf16[256,512]{1,0:T(8,128)(2,1)} %collective-permute-done.13.pa_ref), channel_id=1, source_target_pairs={{4,0},{8,12},{5,1},{9,13},{6,2},{10,14},{7,3},{11,15},{20,16},{24,... | collective-permute-start | bytes 786440 | tf_op jit(solution)/shard_map/ppermute | solution.py:233
  15.2 2.2 %collective-permute-done.6.pair_ref = bf16[256,512]{1,0:T(8,128)(2,1)} collective-permute-done((bf16[256,512]{1,0:T(8,128)(2,1)S(1)}, bf16[256,512]{1,0:T(8,128)(2,1)}, u32[]{:S(2)}, u32[]{:S(2)}) %collective-permute-start.6) | collective-permute-done | bytes 262176 | tf_op jit(solution)/shard_map/ppermute | solution.py:230
  17.3 1.4 %collective-permute-start.8 = (bf16[256,512]{1,0:T(8,128)(2,1)}, bf16[256,512]{1,0:T(8,128)(2,1)}, u32[]{:S(2)}, u32[]{:S(2)}) collective-permute-start(bf16[256,512]{1,0:T(8,128)(2,1)} %collective-permute-done.6.pair_ref), channel_id=1, source_target_pairs={{4,8},{8,4},{5,9},{9,5},{6,10},{10,6},{7,11},{11,7},{20,24},{24,20... | collective-permute-start | bytes 786440 | tf_op jit(solution)/shard_map/ppermute | solution.py:232
  18.7 1.4 %compare_select_fusion = s32[4]{0:T(128)S(1)} fusion(pred[]{:T(512)S(6)} %or.3, s32[2]{0:T(128)S(1)} %slice.43, s32[1]{0:T(128)} %get-tuple-element.33, s32[1]{0:T(128)} %get-tuple-element.32, s32[4]{0:T(128)S(1)} %copy-done.8, pred[]{:T(512)S(6)} %lt.13), kind=kLoop, calls=%fused_computation.12 | loop fusion | flops 28 | bytes 50 | tf_op jit(solution)/shard_map/select_n | solution.py:207
  20.0 1.3 %collective-permute-start.16 = (bf16[256,512]{1,0:T(8,128)(2,1)}, bf16[256,512]{1,0:T(8,128)(2,1)}, u32[]{:S(2)}, u32[]{:S(2)}) collective-permute-start(bf16[256,512]{1,0:T(8,128)(2,1)} %collective-permute-done.14.pb_ref), channel_id=1, source_target_pairs={{4,0},{8,12},{5,1},{9,13},{6,2},{10,14},{7,3},{11,15},{20,16},{24,... | collective-permute-start | bytes 786440 | tf_op jit(solution)/shard_map/ppermute | solution.py:234
  21.4 25.5 %all-gather.1 = s32[8,32,2]{1,2,0:T(2,128)S(1)} all-gather(s32[1,32,2]{1,2,0:T(2,128)S(1)} %bitcast.22), channel_id=2, replica_groups=mesh['groups'=2,'space'=4,'tm'=2,'head'=2] {'space','tm'}, dimensions={0}, use_global_device_ids=true | all-gather | bytes 2304 | tf_op jit(solution)/shard_map/all_gather | solution.py:201
  47.6 1.4 %collective-permute-start.1 = (bf16[256,512]{1,0:T(8,128)(2,1)S(1)}, bf16[256,512]{1,0:T(8,128)(2,1)}, u32[]{:S(2)}, u32[]{:S(2)}) collective-permute-start(bf16[256,512]{1,0:T(8,128)(2,1)S(1)} %pad_maximum_fusion.own_ref), channel_id=1, source_target_pairs={{4,8},{8,4},{5,9},{9,5},{6,10},{10,6},{7,11},{11,7},{20,24},{24,20... | collective-permute-start | bytes 786440 | tf_op jit(solution)/shard_map/ppermute | solution.py:231
  48.9 1.3 %collective-permute-start.9 = (bf16[256,512]{1,0:T(8,128)(2,1)}, bf16[256,512]{1,0:T(8,128)(2,1)}, u32[]{:S(2)}, u32[]{:S(2)}) collective-permute-start(bf16[256,512]{1,0:T(8,128)(2,1)} %collective-permute-done.7.pa_ref), channel_id=1, source_target_pairs={{4,0},{8,12},{5,1},{9,13},{6,2},{10,14},{7,3},{11,15},{20,16},{24,... | collective-permute-start | bytes 786440 | tf_op jit(solution)/shard_map/ppermute | solution.py:233
  50.2 1.4 %collective-permute-start.2 = (bf16[256,512]{1,0:T(8,128)(2,1)S(1)}, bf16[256,512]{1,0:T(8,128)(2,1)}, u32[]{:S(2)}, u32[]{:S(2)}) collective-permute-start(bf16[256,512]{1,0:T(8,128)(2,1)S(1)} %collective-permute-done.pair_ref), channel_id=1, source_target_pairs={{4,8},{8,4},{5,9},{9,5},{6,10},{10,6},{7,11},{11,7},{20,24},{24,20... | collective-permute-start | bytes 786440 | tf_op jit(solution)/shard_map/ppermute | solution.py:232
  51.6 1.3 %collective-permute-start.10 = (bf16[256,512]{1,0:T(8,128)(2,1)}, bf16[256,512]{1,0:T(8,128)(2,1)}, u32[]{:S(2)}, u32[]{:S(2)}) collective-permute-start(bf16[256,512]{1,0:T(8,128)(2,1)} %collective-permute-done.8.pb_ref), channel_id=1, source_target_pairs={{4,0},{8,12},{5,1},{9,13},{6,2},{10,14},{7,3},{11,15},{20,16},{24,... | collective-permute-start | bytes 786440 | tf_op jit(solution)/shard_map/ppermute | solution.py:234
  53.7 1.5 %copy.14.hits_ref = f32[16,128]{1,0:T(8,128)} copy(f32[16,128]{0,1:T(8,128)} %bitcast.15) | data formatting | bytes 16384 | tf_op jit(solution)/shard_map/reshape | solution.py:220
  55.2 1.7 %places.1 = (bf16[512,128]{1,0:T(8,128)(2,1)}, bf16[512,128]{1,0:T(8,128)(2,1)}) custom-call(f32[16,128]{1,0:T(8,128)} %copy.14.hits_ref), custom_call_target="tpu_custom_call" | custom-call | tf_op jit(solution)/shard_map/places/pallas_call | solution.py:221
  56.9 0.9 copy-done.3
  57.8 1.8 %pick0.1 = (bf16[512,512]{1,0:T(8,128)(2,1)S(1)}, bf16[512,512]{1,0:T(8,128)(2,1)S(1)}) custom-call(bf16[512,128]{1,0:T(8,128)(2,1)S(1)} %copy-done.3, bf16[256,512]{1,0:T(8,128)(2,1)S(1)} %pad_maximum_fusion.2.own_ref, bf16[256,512]{1,0:T(8,128)(2,1)} %collective-permute-done.12.pair_ref, bf16[256,512]{1,0:T(8,128)(2,1)} %collective-permute-done.13.pa_ref, ...), custom_call_target="tpu_custom_call" | custom-call | flops 134217728 | bytes 2097152 | tf_op jit(solution)/shard_map/pick0/pallas_call | solution.py:162
  59.8 18.1 %all_gather.9 = bf16[2,64,1536]{2,1,0:T(8,128)(2,1)S(1)} all-gather(bf16[2,16,1536]{2,1,0:T(8,128)(2,1)S(1)} %pad_maximum_fusion.3), channel_id=1, replica_groups=mesh['groups'=2,'space'=4,'tm'=2,'head'=2] {'space'}, dimensions={1}, use_global_device_ids=true | all-gather | bytes 491520 | tf_op jit(solution)/shard_map/all_gather | solution.py:202
  77.9 1.3 %collective-permute-start.3 = (bf16[256,512]{1,0:T(8,128)(2,1)}, bf16[256,512]{1,0:T(8,128)(2,1)S(1)}, u32[]{:S(2)}, u32[]{:S(2)}) collective-permute-start(bf16[256,512]{1,0:T(8,128)(2,1)} %collective-permute-done.1.pa_ref), channel_id=1, source_target_pairs={{4,0},{8,12},{5,1},{9,13},{6,2},{10,14},{7,3},{11,15},{20,16},{24,... | collective-permute-start | bytes 786440 | tf_op jit(solution)/shard_map/ppermute | solution.py:233
  79.2 1.3 %collective-permute-start.4 = (bf16[256,512]{1,0:T(8,128)(2,1)}, bf16[256,512]{1,0:T(8,128)(2,1)S(1)}, u32[]{:S(2)}, u32[]{:S(2)}) collective-permute-start(bf16[256,512]{1,0:T(8,128)(2,1)} %collective-permute-done.2.pb_ref), channel_id=1, source_target_pairs={{4,0},{8,12},{5,1},{9,13},{6,2},{10,14},{7,3},{11,15},{20,16},{24,... | collective-permute-start | bytes 786440 | tf_op jit(solution)/shard_map/ppermute | solution.py:234
  80.5 1.7 %pick1.1 = (bf16[512,512]{1,0:T(8,128)(2,1)S(1)}, bf16[512,512]{1,0:T(8,128)(2,1)S(1)}) custom-call(bf16[512,128]{1,0:T(8,128)(2,1)S(1)} %copy-done.3, bf16[256,512]{1,0:T(8,128)(2,1)S(1)} %pad_maximum_fusion.1.own_ref, bf16[256,512]{1,0:T(8,128)(2,1)} %collective-permute-done.6.pair_ref, bf16[256,512]{1,0:T(8,128)(2,1)} %collective-permute-done.7.pa_ref, ...), custom_call_target="tpu_custom_call" | custom-call | flops 134217728 | bytes 2097152 | tf_op jit(solution)/shard_map/pick1/pallas_call | solution.py:162
  82.2 1.9 %collective-permute-start.11 = (bf16[512,512]{1,0:T(8,128)(2,1)S(1)}, bf16[512,512]{1,0:T(8,128)(2,1)S(1)}, u32[]{:S(2)}, u32[]{:S(2)}) collective-permute-start(bf16[512,512]{1,0:T(8,128)(2,1)S(1)} %get-tuple-element.18), channel_id=1, source_target_pairs={{0,2},{2,0},{1,3},{3,1},{4,6},{6,4},{5,7},{7,5},{8,10},{10,8},{9,1... | collective-permute-start | bytes 1572872 | tf_op jit(solution)/shard_map/ppermute | solution.py:238
  84.2 2.2 %collective-permute-done.3.qa_ref = bf16[256,512]{1,0:T(8,128)(2,1)S(1)} collective-permute-done((bf16[256,512]{1,0:T(8,128)(2,1)}, bf16[256,512]{1,0:T(8,128)(2,1)S(1)}, u32[]{:S(2)}, u32[]{:S(2)}) %collective-permute-start.3) | collective-permute-done | bytes 262176 | tf_op jit(solution)/shard_map/ppermute | solution.py:233
  86.4 2.8 %collective-permute-done.4.qb_ref = bf16[256,512]{1,0:T(8,128)(2,1)S(1)} collective-permute-done((bf16[256,512]{1,0:T(8,128)(2,1)}, bf16[256,512]{1,0:T(8,128)(2,1)S(1)}, u32[]{:S(2)}, u32[]{:S(2)}) %collective-permute-start.4) | collective-permute-done | bytes 262176 | tf_op jit(solution)/shard_map/ppermute | solution.py:234
  89.2 1.4 %pick2.1 = (bf16[512,512]{1,0:T(8,128)(2,1)S(1)}, bf16[512,512]{1,0:T(8,128)(2,1)S(1)}) custom-call(bf16[512,128]{1,0:T(8,128)(2,1)S(1)} %copy-done.3, bf16[256,512]{1,0:T(8,128)(2,1)S(1)} %pad_maximum_fusion.own_ref, bf16[256,512]{1,0:T(8,128)(2,1)S(1)} %collective-permute-done.pair_ref, bf16[256,512]{1,0:T(8,128)(2,1)} %collective-permute-done.1.pa_ref, ...), custom_call_target="tpu_custom_call" | custom-call | flops 134217728 | bytes 2097152 | tf_op jit(solution)/shard_map/pick2/pallas_call | solution.py:162
  90.6 1.9 %collective-permute-start.5 = (bf16[512,512]{1,0:T(8,128)(2,1)S(1)}, bf16[512,512]{1,0:T(8,128)(2,1)S(1)}, u32[]{:S(2)}, u32[]{:S(2)}) collective-permute-start(bf16[512,512]{1,0:T(8,128)(2,1)S(1)} %get-tuple-element.16), channel_id=1, source_target_pairs={{0,2},{2,0},{1,3},{3,1},{4,6},{6,4},{5,7},{7,5},{8,10},{10,8},{9,1... | collective-permute-start | bytes 1572872 | tf_op jit(solution)/shard_map/ppermute | solution.py:238
  93.5 9.8 %attention0.1.refs_8_ = bf16[768,1536]{1,0:T(8,128)(2,1)} custom-call(bf16[768,1536]{1,0:T(8,128)(2,1)S(1)} %copy-done.2, bf16[768,1536]{1,0:T(8,128)(2,1)S(1)} %copy-done, bf16[768,1536]{1,0:T(8,128)(2,1)S(1)} %copy-done.1, bf16[64,1536]{1,0:T(8,128)(2,1)S(1)} %get-tuple-element.31.refs_3_, bf16[64,1536]{1,0:T(8,128)(2,1)S(1)} %get-tuple-element.30.refs_4_, ...), custom_call_target="tpu_custom_call" | custom-call | flops 3170893824 | bytes 4194304 | tf_op jit(solution)/shard_map/attention0/pallas_call | solution.py:94
  103.3 9.8 %attention1.1.refs_8_ = bf16[768,1536]{1,0:T(8,128)(2,1)} custom-call(bf16[768,1536]{1,0:T(8,128)(2,1)S(1)} %copy-done.2, bf16[768,1536]{1,0:T(8,128)(2,1)S(1)} %copy-done, bf16[768,1536]{1,0:T(8,128)(2,1)S(1)} %copy-done.1, bf16[64,1536]{1,0:T(8,128)(2,1)S(1)} %get-tuple-element.31.refs_3_, ...), custom_call_target="tpu_custom_call", output_to_operand_aliasing={{}: (8, {})} | custom-call | flops 3170893824 | bytes 4194304 | tf_op jit(solution)/shard_map/attention1/pallas_call | solution.py:94
  113.2 9.8 %attention2.1 = bf16[768,1536]{1,0:T(8,128)(2,1)} custom-call(bf16[768,1536]{1,0:T(8,128)(2,1)S(1)} %copy-done.2, bf16[768,1536]{1,0:T(8,128)(2,1)S(1)} %copy-done, bf16[768,1536]{1,0:T(8,128)(2,1)S(1)} %copy-done.1, bf16[64,1536]{1,0:T(8,128)(2,1)S(1)} %get-tuple-element.31.refs_3_, ...), custom_call_target="tpu_custom_call", output_to_operand_aliasing={{}: (8, {})} | custom-call | flops 3170893824 | bytes 4194304 | tf_op jit(solution)/shard_map/attention2/pallas_call | solution.py:94
  (49 shorter events, 3.9 us)
Async XLA Ops:
  0.0 11.7 %copy-start.8 = (s32[4]{0:T(128)S(1)}, s32[4]{0:T(128)}, u32[]{:S(2)}) copy-start(s32[4]{0:T(128)} %constant.32.clone) | copy-start | bytes 52
  0.0 11.6 %copy-start.6 = (bf16[16,1536]{1,0:T(8,128)(2,1)S(1)}, bf16[16,1536]{1,0:T(8,128)(2,1)}, u32[]{:S(2)}) copy-start(bf16[16,1536]{1,0:T(8,128)(2,1)} %param.11) | copy-start | bytes 147460
  0.0 11.6 %copy-start.5 = (bf16[16,1536]{1,0:T(8,128)(2,1)S(1)}, bf16[16,1536]{1,0:T(8,128)(2,1)}, u32[]{:S(2)}) copy-start(bf16[16,1536]{1,0:T(8,128)(2,1)} %param.12) | copy-start | bytes 147460
  0.0 21.4 %copy-start.7 = (s32[32,2]{0,1:T(2,128)S(1)}, s32[32,2]{0,1:T(2,128)}, u32[]{:S(2)}) copy-start(s32[32,2]{0,1:T(2,128)} %param.13) | copy-start | bytes 772
  1.3 10.4 %collective-permute-start.12 = (bf16[256,512]{1,0:T(8,128)(2,1)S(1)}, bf16[256,512]{1,0:T(8,128)(2,1)}, u32[]{:S(2)}, u32[]{:S(2)}) collective-permute-start(bf16[256,512]{1,0:T(8,128)(2,1)S(1)} %pad_maximum_fusion.2.own_ref), channel_id=1, source_target_pairs={{0,4},{4,0},{8,12},{12,8},{1,5},{5,1},{9,13},{13,9},{2,6},{6,2},{1... | collective-permute-start | bytes 786440 | tf_op jit(solution)/shard_map/ppermute | solution.py:230
  4.5 9.4 %collective-permute-start.13 = (bf16[256,512]{1,0:T(8,128)(2,1)S(1)}, bf16[256,512]{1,0:T(8,128)(2,1)}, u32[]{:S(2)}, u32[]{:S(2)}) collective-permute-start(bf16[256,512]{1,0:T(8,128)(2,1)S(1)} %pad_maximum_fusion.2.own_ref), channel_id=1, source_target_pairs={{4,8},{8,4},{5,9},{9,5},{6,10},{10,6},{7,11},{11,7},{20,24},{24,20... | collective-permute-start | bytes 786440 | tf_op jit(solution)/shard_map/ppermute | solution.py:231
  5.8 11.5 %collective-permute-start.6 = (bf16[256,512]{1,0:T(8,128)(2,1)S(1)}, bf16[256,512]{1,0:T(8,128)(2,1)}, u32[]{:S(2)}, u32[]{:S(2)}) collective-permute-start(bf16[256,512]{1,0:T(8,128)(2,1)S(1)} %pad_maximum_fusion.1.own_ref), channel_id=1, source_target_pairs={{0,4},{4,0},{8,12},{12,8},{1,5},{5,1},{9,13},{13,9},{2,6},{6,2},{1... | collective-permute-start | bytes 786440 | tf_op jit(solution)/shard_map/ppermute | solution.py:230
  9.6 38.0 %collective-permute-start.7 = (bf16[256,512]{1,0:T(8,128)(2,1)S(1)}, bf16[256,512]{1,0:T(8,128)(2,1)}, u32[]{:S(2)}, u32[]{:S(2)}) collective-permute-start(bf16[256,512]{1,0:T(8,128)(2,1)S(1)} %pad_maximum_fusion.1.own_ref), channel_id=1, source_target_pairs={{4,8},{8,4},{5,9},{9,5},{6,10},{10,6},{7,11},{11,7},{20,24},{24,20... | collective-permute-start | bytes 786440 | tf_op jit(solution)/shard_map/ppermute | solution.py:231
  11.0 38.0 %collective-permute-start = (bf16[256,512]{1,0:T(8,128)(2,1)S(1)}, bf16[256,512]{1,0:T(8,128)(2,1)S(1)}, u32[]{:S(2)}, u32[]{:S(2)}) collective-permute-start(bf16[256,512]{1,0:T(8,128)(2,1)S(1)} %pad_maximum_fusion.own_ref), channel_id=1, source_target_pairs={{0,4},{4,0},{8,12},{12,8},{1,5},{5,1},{9,13},{13,9},{2,6},{6,2},{1... | collective-permute-start | bytes 786440 | tf_op jit(solution)/shard_map/ppermute | solution.py:230
  11.7 80.9 %copy-start.2 = (bf16[768,1536]{1,0:T(8,128)(2,1)S(1)}, bf16[768,1536]{1,0:T(8,128)(2,1)}, u32[]{:S(2)}) copy-start(bf16[768,1536]{1,0:T(8,128)(2,1)} %refs_0_.5) | copy-start | bytes 7077892
  11.7 8.3 %collective-permute-start.14 = (bf16[256,512]{1,0:T(8,128)(2,1)}, bf16[256,512]{1,0:T(8,128)(2,1)}, u32[]{:S(2)}, u32[]{:S(2)}) collective-permute-start(bf16[256,512]{1,0:T(8,128)(2,1)} %collective-permute-done.12.pair_ref), channel_id=1, source_target_pairs={{4,8},{8,4},{5,9},{9,5},{6,10},{10,6},{7,11},{11,7},{20,24},{24,20... | collective-permute-start | bytes 786440 | tf_op jit(solution)/shard_map/ppermute | solution.py:232
  13.9 36.4 %collective-permute-start.15 = (bf16[256,512]{1,0:T(8,128)(2,1)}, bf16[256,512]{1,0:T(8,128)(2,1)}, u32[]{:S(2)}, u32[]{:S(2)}) collective-permute-start(bf16[256,512]{1,0:T(8,128)(2,1)} %collective-permute-done.13.pa_ref), channel_id=1, source_target_pairs={{4,0},{8,12},{5,1},{9,13},{6,2},{10,14},{7,3},{11,15},{20,16},{24,... | collective-permute-start | bytes 786440 | tf_op jit(solution)/shard_map/ppermute | solution.py:233
  17.3 34.3 %collective-permute-start.8 = (bf16[256,512]{1,0:T(8,128)(2,1)}, bf16[256,512]{1,0:T(8,128)(2,1)}, u32[]{:S(2)}, u32[]{:S(2)}) collective-permute-start(bf16[256,512]{1,0:T(8,128)(2,1)} %collective-permute-done.6.pair_ref), channel_id=1, source_target_pairs={{4,8},{8,4},{5,9},{9,5},{6,10},{10,6},{7,11},{11,7},{20,24},{24,20... | collective-permute-start | bytes 786440 | tf_op jit(solution)/shard_map/ppermute | solution.py:232
  20.0 36.9 %collective-permute-start.16 = (bf16[256,512]{1,0:T(8,128)(2,1)}, bf16[256,512]{1,0:T(8,128)(2,1)}, u32[]{:S(2)}, u32[]{:S(2)}) collective-permute-start(bf16[256,512]{1,0:T(8,128)(2,1)} %collective-permute-done.14.pb_ref), channel_id=1, source_target_pairs={{4,0},{8,12},{5,1},{9,13},{6,2},{10,14},{7,3},{11,15},{20,16},{24,... | collective-permute-start | bytes 786440 | tf_op jit(solution)/shard_map/ppermute | solution.py:234
  47.6 30.3 %collective-permute-start.1 = (bf16[256,512]{1,0:T(8,128)(2,1)S(1)}, bf16[256,512]{1,0:T(8,128)(2,1)}, u32[]{:S(2)}, u32[]{:S(2)}) collective-permute-start(bf16[256,512]{1,0:T(8,128)(2,1)S(1)} %pad_maximum_fusion.own_ref), channel_id=1, source_target_pairs={{4,8},{8,4},{5,9},{9,5},{6,10},{10,6},{7,11},{11,7},{20,24},{24,20... | collective-permute-start | bytes 786440 | tf_op jit(solution)/shard_map/ppermute | solution.py:231
  48.9 31.6 %collective-permute-start.9 = (bf16[256,512]{1,0:T(8,128)(2,1)}, bf16[256,512]{1,0:T(8,128)(2,1)}, u32[]{:S(2)}, u32[]{:S(2)}) collective-permute-start(bf16[256,512]{1,0:T(8,128)(2,1)} %collective-permute-done.7.pa_ref), channel_id=1, source_target_pairs={{4,0},{8,12},{5,1},{9,13},{6,2},{10,14},{7,3},{11,15},{20,16},{24,... | collective-permute-start | bytes 786440 | tf_op jit(solution)/shard_map/ppermute | solution.py:233
  50.2 29.0 %collective-permute-start.2 = (bf16[256,512]{1,0:T(8,128)(2,1)S(1)}, bf16[256,512]{1,0:T(8,128)(2,1)}, u32[]{:S(2)}, u32[]{:S(2)}) collective-permute-start(bf16[256,512]{1,0:T(8,128)(2,1)S(1)} %collective-permute-done.pair_ref), channel_id=1, source_target_pairs={{4,8},{8,4},{5,9},{9,5},{6,10},{10,6},{7,11},{11,7},{20,24},{24,20... | collective-permute-start | bytes 786440 | tf_op jit(solution)/shard_map/ppermute | solution.py:232
  51.6 28.9 %collective-permute-start.10 = (bf16[256,512]{1,0:T(8,128)(2,1)}, bf16[256,512]{1,0:T(8,128)(2,1)}, u32[]{:S(2)}, u32[]{:S(2)}) collective-permute-start(bf16[256,512]{1,0:T(8,128)(2,1)} %collective-permute-done.8.pb_ref), channel_id=1, source_target_pairs={{4,0},{8,12},{5,1},{9,13},{6,2},{10,14},{7,3},{11,15},{20,16},{24,... | collective-permute-start | bytes 786440 | tf_op jit(solution)/shard_map/ppermute | solution.py:234
  56.9 0.9 copy-start.3
  57.8 34.7 %copy-start.1 = (bf16[768,1536]{1,0:T(8,128)(2,1)S(1)}, bf16[768,1536]{1,0:T(8,128)(2,1)}, u32[]{:S(2)}) copy-start(bf16[768,1536]{1,0:T(8,128)(2,1)} %refs_2_.5) | copy-start | bytes 7077892
  59.7 32.9 %copy-start = (bf16[768,1536]{1,0:T(8,128)(2,1)S(1)}, bf16[768,1536]{1,0:T(8,128)(2,1)}, u32[]{:S(2)}) copy-start(bf16[768,1536]{1,0:T(8,128)(2,1)} %refs_1_.5) | copy-start | bytes 7077892
  59.7 32.9 %collective-permute-start.17 = (bf16[512,512]{1,0:T(8,128)(2,1)S(1)}, bf16[512,512]{1,0:T(8,128)(2,1)S(1)}, u32[]{:S(2)}, u32[]{:S(2)}) collective-permute-start(bf16[512,512]{1,0:T(8,128)(2,1)S(1)} %get-tuple-element.20), channel_id=1, source_target_pairs={{0,2},{2,0},{1,3},{3,1},{4,6},{6,4},{5,7},{7,5},{8,10},{10,8},{9,1... | collective-permute-start | bytes 1572872 | tf_op jit(solution)/shard_map/ppermute | solution.py:238
  77.9 8.5 %collective-permute-start.3 = (bf16[256,512]{1,0:T(8,128)(2,1)}, bf16[256,512]{1,0:T(8,128)(2,1)S(1)}, u32[]{:S(2)}, u32[]{:S(2)}) collective-permute-start(bf16[256,512]{1,0:T(8,128)(2,1)} %collective-permute-done.1.pa_ref), channel_id=1, source_target_pairs={{4,0},{8,12},{5,1},{9,13},{6,2},{10,14},{7,3},{11,15},{20,16},{24,... | collective-permute-start | bytes 786440 | tf_op jit(solution)/shard_map/ppermute | solution.py:233
  79.2 10.0 %collective-permute-start.4 = (bf16[256,512]{1,0:T(8,128)(2,1)}, bf16[256,512]{1,0:T(8,128)(2,1)S(1)}, u32[]{:S(2)}, u32[]{:S(2)}) collective-permute-start(bf16[256,512]{1,0:T(8,128)(2,1)} %collective-permute-done.2.pb_ref), channel_id=1, source_target_pairs={{4,0},{8,12},{5,1},{9,13},{6,2},{10,14},{7,3},{11,15},{20,16},{24,... | collective-permute-start | bytes 786440 | tf_op jit(solution)/shard_map/ppermute | solution.py:234
  82.2 21.1 %collective-permute-start.11 = (bf16[512,512]{1,0:T(8,128)(2,1)S(1)}, bf16[512,512]{1,0:T(8,128)(2,1)S(1)}, u32[]{:S(2)}, u32[]{:S(2)}) collective-permute-start(bf16[512,512]{1,0:T(8,128)(2,1)S(1)} %get-tuple-element.18), channel_id=1, source_target_pairs={{0,2},{2,0},{1,3},{3,1},{4,6},{6,4},{5,7},{7,5},{8,10},{10,8},{9,1... | collective-permute-start | bytes 1572872 | tf_op jit(solution)/shard_map/ppermute | solution.py:238
  90.6 22.5 %collective-permute-start.5 = (bf16[512,512]{1,0:T(8,128)(2,1)S(1)}, bf16[512,512]{1,0:T(8,128)(2,1)S(1)}, u32[]{:S(2)}, u32[]{:S(2)}) collective-permute-start(bf16[512,512]{1,0:T(8,128)(2,1)S(1)} %get-tuple-element.16), channel_id=1, source_target_pairs={{0,2},{2,0},{1,3},{3,1},{4,6},{6,4},{5,7},{7,5},{8,10},{10,8},{9,1... | collective-permute-start | bytes 1572872 | tf_op jit(solution)/shard_map/ppermute | solution.py:238
  92.6 0.9 copy-start.4

commit v2 on v0

v2 whole, which is shorter than its diff:
```python
import functools
import math

import jax
import jax.numpy as jnp
from jax import lax
from jax.experimental import pallas as pl
from jax.experimental.pallas import tpu as pltpu
from jax.sharding import PartitionSpec as P

HD = 128
FACE_ROWS = 4
HEAD_CUTS = (6, 6)
STEP_HEADS = 2
TILE_Q = 384
VMEM_BYTES = 60 * 1024 * 1024
LOG2E = 1.4426950408889634
BF = jnp.bfloat16
F32 = jnp.float32


def face_selection(face_dest, tile_count, slot_count):
    window_blocks, readers = face_dest.shape
    flat_dest = face_dest.reshape(-1)
    owners = jnp.arange(tile_count, dtype=jnp.int32)
    matches = (flat_dest[:, None] == owners[None, :]).astype(jnp.int32)
    earlier = jnp.cumsum(matches, axis=0) - matches
    slot_rank = jnp.sum(earlier * matches, axis=1)
    target = flat_dest * slot_count + slot_rank
    places = jnp.arange(tile_count * slot_count, dtype=jnp.int32)
    chosen = (places[:, None] == target[None, :]).astype(jnp.float32)
    return jnp.sum(chosen.reshape(tile_count * slot_count, window_blocks, readers), axis=2)


def attention_kernel(settings, line_ref, *refs):
    tok_rows, slot_rows, text_rows, parts, gathered = settings
    q_ref, k_ref, v_ref = refs[:3]
    arrays = parts // 2 if gathered else parts
    part_refs = refs[3 : 3 + arrays]
    if gathered:
        each = part_refs[0].shape[0] // 2
        part_refs = [part.at[half * each : (half + 1) * each, :] for part in part_refs for half in range(2)]
    mark_refs = refs[3 + arrays : 3 + arrays + parts]
    extra = refs[3 + arrays + parts : -4]
    out_ref, key_rows, value_rows, flag_rows = refs[-4:]
    scale = LOG2E / math.sqrt(HD)
    total = key_rows.shape[1]

    @pl.when(pl.program_id(0) == 0)
    def _():
        for place, mark in enumerate(mark_refs):
            rows = slice(place * slot_rows, (place + 1) * slot_rows)
            if gathered:
                hits = jnp.where(mark[...].astype(F32) == line_ref[1].astype(F32), 1.0, 0.0)
                count = jnp.sum(jnp.max(hits, axis=0, keepdims=True), axis=1, keepdims=True)
                slot = lax.broadcasted_iota(jnp.int32, (slot_rows, HD), 0).astype(F32)
                flag_rows[rows, :] = (slot < count).astype(F32).astype(BF)
            else:
                flag_rows[rows, :] = mark[...]
        for sub in range(STEP_HEADS):
            value_rows[sub, :, HD:] = jnp.ones((total, HD), BF)
            value_rows[sub, tok_rows : tok_rows + parts * slot_rows, HD:] = flag_rows[...]

    for sub in range(STEP_HEADS):
        cols = slice(sub * HD, (sub + 1) * HD)
        key_rows[sub, 0:tok_rows, :] = k_ref[:, cols]
        value_rows[sub, 0:tok_rows, 0:HD] = v_ref[:, cols]
        at = tok_rows
        spare = k_ref[0:1, cols]
        for place, part in enumerate(part_refs):
            flags = flag_rows[place * slot_rows : (place + 1) * slot_rows, :]
            key_rows[sub, at : at + slot_rows, :] = jnp.where(flags > 0, part[0:slot_rows, cols], spare)
            value_rows[sub, at : at + slot_rows, 0:HD] = part[slot_rows : 2 * slot_rows, cols]
            at += slot_rows
        if gathered:
            front = line_ref[0] == 0
            half = parts // 2
            for mine, came in zip(part_refs[:half], part_refs[half:]):
                kept = mine[2 * slot_rows : 2 * slot_rows + text_rows, cols]
                brought = came[2 * slot_rows : 2 * slot_rows + text_rows, cols]
                key_rows[sub, at : at + text_rows, :] = jnp.where(front, kept, brought)
                value_rows[sub, at : at + text_rows, 0:HD] = jnp.where(front, brought, kept)
                at += text_rows
        else:
            key_rows[sub, at:, :] = extra[0][:, cols]
            value_rows[sub, at:, 0:HD] = extra[1][:, cols]
        for start in range(0, tok_rows, TILE_Q):
            rows = slice(start, start + TILE_Q)
            scores = lax.dot_general(
                q_ref[rows, cols], key_rows[sub], (((1,), (1,)), ((), ())), preferred_element_type=F32
            )
            top = jnp.max(scores, axis=1, keepdims=True)
            weights = jnp.exp2((scores - top) * scale).astype(BF)
            mixed = jnp.dot(weights, value_rows[sub], preferred_element_type=F32)
            out_ref[rows, cols] = (mixed[:, :HD] / mixed[:, HD:]).astype(BF)


def attention(first, heads, line, queries, keys, values, parts, marks, text, slot_rows, text_rows, total, out, after):
    tok_rows, width = queries.shape
    wide = STEP_HEADS * HD
    col = lambda h, s: (0, first // STEP_HEADS + h)
    here = lambda h, s: (0, h)
    specs = [pl.BlockSpec((tok_rows, wide), col)] * 3
    operands = [line, queries, keys, values]
    for part in parts:
        specs.append(pl.BlockSpec((part.shape[0], wide), col if part.shape[1] == width else here))
        operands.append(part)
    for mark in marks:
        if text:
            specs.append(pl.BlockSpec((slot_rows, HD), lambda h, s: (0, 0)))
        else:
            for at in (mark.shape[0] // 32 - 1, mark.shape[0] // 16 - 1):
                specs.append(pl.BlockSpec((16, HD), lambda h, s, at=at: (at, 0)))
            operands.append(mark)
        operands.append(mark)
    for words in text:
        specs.append(pl.BlockSpec((words.shape[0], wide), col))
        operands.append(words)
    aliases = {}
    if out is not None:
        aliases = {len(operands): 0}
        specs.append(pl.BlockSpec(memory_space=pl.ANY))
        operands.append(out)
    for array in after:
        specs.append(pl.BlockSpec(memory_space=pl.ANY))
        operands.append(array)
    settings = (tok_rows, slot_rows, text_rows, len(parts) * (1 if text else 2), not text)
    return pl.pallas_call(
        functools.partial(attention_kernel, settings),
        grid_spec=pltpu.PrefetchScalarGridSpec(
            num_scalar_prefetch=1,
            grid=(heads // STEP_HEADS,),
            in_specs=specs,
            out_specs=pl.BlockSpec((tok_rows, wide), col),
            scratch_shapes=[
                pltpu.VMEM((STEP_HEADS, total, HD), BF),
                pltpu.VMEM((STEP_HEADS, total, 2 * HD), BF),
                pltpu.VMEM((settings[3] * slot_rows, HD), BF),
            ],
        ),
        out_shape=jax.ShapeDtypeStruct((tok_rows, width), BF),
        input_output_aliases=aliases,
        compiler_params=pltpu.CompilerParams(vmem_limit_bytes=VMEM_BYTES),
        cost_estimate=pl.CostEstimate(
            flops=heads * HD * tok_rows,
            bytes_accessed=heads * HD * 2 * tok_rows,
            transcendentals=0,
        ),
        name="attention%d" % first,
    )(*operands)


def pick_kernel(slot_rows, span, counts, line_ref, *refs):
    blocks = sum(counts)
    slab_refs, held_refs, (mine_ref, sent_ref) = refs[:blocks], refs[blocks : 2 * blocks], refs[-2:]
    row = lax.broadcasted_iota(jnp.int32, (span, span), 0)
    column = lax.broadcasted_iota(jnp.int32, (span, span), 1)
    before = ((row < column) & (row % FACE_ROWS == column % FACE_ROWS)).astype(F32).astype(BF)
    slot = lax.broadcasted_iota(jnp.int32, (slot_rows, span), 0).astype(F32)
    member = (lax.broadcasted_iota(jnp.int32, (1, span), 1) % FACE_ROWS).astype(F32)
    at = 0
    base = 0
    for count in counts:
        slabs, held = slab_refs[at : at + count], held_refs[at : at + count]
        at += count

        def get(start, rows):
            got = held[0][start : start + rows, :]
            return got if count == 1 else got + held[1][start : start + rows, :]

        dest = slabs[0][...] if count == 1 else slabs[0][...] + slabs[1][...]
        dest = dest.astype(F32)
        rest = held[0].shape[0] - 2 * span
        keys, values = get(0, span), get(span, span)
        for side, target_ref in enumerate((mine_ref, sent_ref)):
            hits = jnp.where(dest == line_ref[1 + side].astype(F32), 1.0, 0.0)
            hits = jnp.max(hits, axis=0, keepdims=True)
            rank = jnp.dot(
                jnp.broadcast_to(hits, (16, span)).astype(BF), before, preferred_element_type=F32
            )[0:1, :]
            target = jnp.where(hits > 0, rank * FACE_ROWS + member, -1.0)
            choose = (slot == target).astype(F32).astype(BF)
            for part, rows in enumerate((keys, values)):
                got = jnp.dot(choose, rows, preferred_element_type=F32).astype(BF)
                here = base + part * slot_rows
                target_ref[here : here + slot_rows, :] = got
            here = base + 2 * slot_rows
            target_ref[here : here + rest, :] = get(2 * span, rest)
        base += 2 * slot_rows + rest


def pick(label, slot_rows, span, line, sources, slabs, after):
    counts = tuple(len(source) for source in sources)
    arrays = [array for source in sources for array in source]
    marks = [array for source in slabs for array in source]
    rows, width = arrays[0].shape
    each = rows - 2 * span + 2 * slot_rows
    shape = jax.ShapeDtypeStruct((each * len(sources), width), BF)
    at = marks[0].shape[0] // 16 - 1
    zero = lambda i, s: (0, 0)
    return pl.pallas_call(
        functools.partial(pick_kernel, slot_rows, span, counts),
        grid_spec=pltpu.PrefetchScalarGridSpec(
            num_scalar_prefetch=1,
            grid=(1,),
            in_specs=[pl.BlockSpec((16, span), lambda i, s: (at, 0))] * len(marks)
            + [pl.BlockSpec(a.shape, zero) for a in arrays]
            + [pl.BlockSpec(memory_space=pl.ANY)] * len(after),
            out_specs=(pl.BlockSpec(shape.shape, zero),) * 2,
        ),
        out_shape=(shape, shape),
        compiler_params=pltpu.CompilerParams(vmem_limit_bytes=VMEM_BYTES),
        cost_estimate=pl.CostEstimate(
            flops=8 * len(sources) * slot_rows * span * width,
            bytes_accessed=6 * len(sources) * span * width * 2,
            transcendentals=0,
        ),
        name="pick_" + label,
    )(line, *marks, *arrays, *after)


def chained(queries, keys, values, text_keys, text_values, face_dest):
    spaces = lax.axis_size("space")
    frames = lax.axis_size("tm")
    tile_count = spaces * frames
    window_blocks, readers = face_dest.shape
    tok_rows, width = keys.shape
    text = text_keys.shape[0]
    slot_count = max(2, 2 * window_blocks * readers // tile_count)
    span = window_blocks * FACE_ROWS
    slot_rows = slot_count * FACE_ROWS
    z = lax.axis_index("space")
    x = lax.axis_index("tm")
    line = jnp.stack([x, z * frames + x, z * frames + 1 - x]).astype(jnp.int32)

    ends = [(0, 1), (1, 0), (2, 3), (3, 2)]
    inner = [(1, 2), (2, 1)]
    outward = [(1, 0), (2, 3)]
    swap = [(0, 1), (1, 0)]
    dest = jnp.repeat(face_dest.T, FACE_ROWS, axis=1)
    dest = jnp.concatenate([dest] * (16 // readers), axis=0).astype(BF)
    words = jnp.where(x == 0, text_keys, text_values)
    slab = jnp.pad(dest, ((0, 0), (0, HEAD_CUTS[0] * HD - span)))
    bundles = []
    column = 0
    for heads in HEAD_CUTS:
        cols = slice(column, column + heads * HD)
        rows = [keys[:span, cols], values[:span, cols], words[:, cols]]
        bundles.append(jnp.concatenate(rows + [slab] if column == 0 else rows, axis=0))
        column += heads * HD
    def take(label, sources, slabs, after):
        kept, sent = pick(label, slot_rows, span, line, sources, slabs, after)
        return kept, lax.ppermute(sent, "tm", swap)

    held, near = [], []
    for g, own in enumerate(bundles):
        pair = lax.ppermute(own, "space", ends)
        pa = lax.ppermute(own, "space", inner)
        if g == 0:
            slabs = ((own,), (pair,))
            near.append(take("near0", slabs, slabs, ()))
        pb = lax.ppermute(pair, "space", inner)
        qa = lax.ppermute(pa, "space", outward)
        if g > 0:
            near.append(take("near%d" % g, ((own,), (pair,)), slabs, (qa,)))
        beyond, _ = lax.optimization_barrier((pb, near[0][0])) if g > 0 else (pb, None)
        qb = lax.ppermute(beyond, "space", outward)
        held.append(((pa, qa), (pb, qb)))
    count = len(HEAD_CUTS)
    far = [take("far%d" % g, held[g], held[0], ()) for g in range(count)]
    out = None
    first = 0
    total = tok_rows + tile_count * slot_rows + spaces * text
    marks = [near[0][0], far[0][0], near[0][1], far[0][1]]
    for g, heads in enumerate(HEAD_CUTS):
        parts = [near[g][0], far[g][0], near[g][1], far[g][1]]
        after = (far[-1][0],) if g == 0 else ()
        out = attention(
            first, heads, line, queries, keys, values, parts, marks, (), slot_rows, text, total, out, after
        )
        first += heads
    return out


def exchanged(queries, keys, values, text_keys, text_values, face_dest):
    spaces = lax.axis_size("space")
    frames = lax.axis_size("tm")
    tile_count = spaces * frames
    window_blocks, readers = face_dest.shape
    tok_rows, width = keys.shape
    slot_count = max(2, 2 * window_blocks * readers // tile_count)
    span = window_blocks * FACE_ROWS
    slot_rows = slot_count * FACE_ROWS
    chosen = face_selection(face_dest, tile_count, slot_count)

    def exchange(rows):
        blocks = rows[:span].reshape(window_blocks, FACE_ROWS * width)
        send = jnp.dot(chosen.astype(BF), blocks, preferred_element_type=F32).astype(BF)
        send = send.reshape(tile_count, slot_rows, width)
        got = lax.all_to_all(send, ("space", "tm"), split_axis=0, concat_axis=0, tiled=True)
        return got.reshape(-1, width)

    live_slots = jnp.sum(chosen, axis=1).astype(BF).reshape(tile_count, slot_count)
    got_live = lax.all_to_all(live_slots, ("space", "tm"), split_axis=0, concat_axis=0, tiled=True)
    live = jnp.repeat(got_live.reshape(-1, 1), FACE_ROWS, axis=0)
    live = jnp.broadcast_to(live, (live.shape[0], HD))
    received = jnp.concatenate([exchange(keys), exchange(values)], axis=0)
    text_k = lax.all_gather(text_keys, "space", axis=0, tiled=True)
    text_v = lax.all_gather(text_values, "space", axis=0, tiled=True)
    rows = live.shape[0]
    total = tok_rows + rows + text_k.shape[0]
    line = lax.axis_index("tm").reshape(1).astype(jnp.int32)
    return attention(
        0, width // HD, line, queries, keys, values, [received], [live], (text_k, text_v), rows, 0, total, None, ()
    )


def on_device(*arrays):
    if lax.axis_size("space") == 4 and lax.axis_size("tm") == 2:
        return chained(*arrays)
    return exchanged(*arrays)


def solution(mesh):
    placed = (
        P(("groups", "space", "tm"), "head"),
        P(("groups", "space", "tm"), "head"),
        P(("groups", "space", "tm"), "head"),
        P(("groups", "space"), "head"),
        P(("groups", "space"), "head"),
        P(("groups", "space", "tm"), None),
    )
    return jax.shard_map(
        on_device,
        mesh=mesh,
        in_specs=placed,
        out_specs=P(("groups", "space", "tm"), "head"),
        check_vma=False,
    )
```

time: 211 us -> 102 us (0.48)
  blocking collectives: 58.7 us -> 0 us
  matrix products: 45.3 us -> 0 us
  Pallas kernels: 0 us -> 40.3 us
  local copies, waits for them, and re-layouts: 32.3 us -> 4.91 us
  other arithmetic: 16 us -> 2.23 us
  loops' own time: 8.62 us -> 0 us
  starting transfers between devices: 14.5 us -> 18.8 us
    all_gather x2 -> x0, blocking collectives: 58.7 us -> none  [the longest x1 44.9 us: on_device(): lax.all_gather(text_keys, 'space', axis=0, tiled=True)]
    dot_general x26 -> x0, matrix products: 45.3 us -> none  [the longest x12 21.7 us: one_head(): lax.dot_general(query_part, key_part, (((1,), (1,)), ((), ())), preferred...]
    pallas_call x0 -> x6, Pallas kernels: none -> 40.3 us  [the longest x2 25.7 us: attention(): pl.pallas_call(functools.partial(attention_kernel, settings), grid_spec=p...]
    ppermute x0 -> x14, waiting for transfers between devices: none -> 35.5 us  [the longest x2 16.3 us: chained(): pair = lax.ppermute(own, 'space', ends)]
    all_to_all x3 -> x0, waiting for transfers between devices: 34.3 us -> none  [the longest x1 31.7 us: on_device(): lax.all_to_all(send_keys.reshape(tile_count, slot_rows, feature_width), (...]
    ppermute x0 -> x14, starting transfers between devices: none -> 18.8 us  [the longest x4 6.21 us: take(): return (kept, lax.ppermute(sent, 'tm', swap))]
    all_to_all x3 -> x0, starting transfers between devices: 14.5 us -> none  [the longest x1 7.25 us: on_device(): lax.all_to_all(live_slots.reshape(tile_count, slot_count), ('space', 'tm'...]
    dynamic_update_slice x24 -> x0, local copies, waits for them, and re-layouts: 10.2 us -> none  [on_device(): per_head = lax.map(one_head, jnp.arange(head_count, dtype=jnp.int32))]
  transfers between devices with their start and end apart: 3 -> 14, of which waited for: 2 -> 6; matrix products, arithmetic and copies ran while one was open for 7% -> 1% of each run, Pallas kernels for 0% -> 27%
where the time goes in v2:
time: 102 us
  Pallas kernels  40.3 us (40%)
  waiting for transfers between devices  35.5 us (35%)
  starting transfers between devices  18.8 us (18%)
  local copies, waits for them, and re-layouts  4.91 us (5%)
  other arithmetic  2.23 us (2%)
    pallas_call x2, Pallas kernels, attention(): pl.pallas_call(functools.partial(attention_kernel, settings), grid_spec=p...  25.7 us
    ppermute x2, waiting for transfers between devices, chained(): pair = lax.ppermute(own, 'space', ends)  16.3 us
    pallas_call x4, Pallas kernels, pick(): pl.pallas_call(functools.partial(pick_kernel, slot_rows, span, counts), g...  14.6 us
    ppermute x2, waiting for transfers between devices, chained(): qb = lax.ppermute(beyond, 'space', outward)  11.3 us
    ppermute x2, waiting for transfers between devices, chained(): qa = lax.ppermute(pa, 'space', outward)  7.97 us
    ppermute x4, starting transfers between devices, take(): return (kept, lax.ppermute(sent, 'tm', swap))  6.21 us
    unnamed x24, local copies, waits for them, and re-layouts  3.37 us
    ppermute x2, starting transfers between devices, chained(): pair = lax.ppermute(own, 'space', ends)  3.17 us
  transfers between devices with their start and end apart: 14, of which 6 were waited for; matrix products, arithmetic and copies ran while one was open for 1% of the time, Pallas kernels for 27%

profile of v2, /device:TPU:0, one launch (start us, length us, event | category | flops | bytes accessed | tf_op | source)
XLA Modules:
  0.0 101.9 jit_solution(18332863135538554624)
XLA Ops:
  0.0 0.7 convert_bitcast_fusion
  0.9 0.8 broadcast_select_fusion
  1.8 1.3 %fusion.2 = (bf16[128,768]{1,0:T(8,128)(2,1)S(1)}, bf16[128,768]{1,0:T(8,128)(2,1)S(1)}, bf16[128,768]{1,0:T(8,128)(2,1)S(1)}, bf16[128,768]{1,0:T(8,128)(2,1)S(1)}) fusion(bf16[768,1536]{1,0:T(8,128)(2,1)} %refs_1_.3, bf16[768,1536]{1,0:T(8,128)(2,1)} %refs_2_.3), kind=kLoop, calls=%fused_computation.7 | loop fusion | bytes 1572864 | tf_op jit(solution)/shard_map/slice | solution.py:248
  3.1 3.1 %collective-permute-start = (bf16[288,768]{1,0:T(8,128)(2,1)S(1)}, bf16[288,768]{1,0:T(8,128)(2,1)S(1)}, u32[]{:S(2)}, u32[]{:S(2)}) collective-permute-start(bf16[288,768]{1,0:T(8,128)(2,1)S(1)} %fusion.1.refs_0_.refs_2_), channel_id=1, source_target_pairs={{0,4},{4,0},{8,12},{12,8},{1,5},{5,1},{9,13},{13,9},{2,6},{6,2},{1... | collective-permute-start | bytes 1327112 | tf_op jit(solution)/shard_map/ppermute | solution.py:257
  6.3 0.7 collective-permute-start.4
  7.0 10.2 %collective-permute-done.refs_1_.refs_3_ = bf16[288,768]{1,0:T(8,128)(2,1)S(1)} collective-permute-done((bf16[288,768]{1,0:T(8,128)(2,1)S(1)}, bf16[288,768]{1,0:T(8,128)(2,1)S(1)}, u32[]{:S(2)}, u32[]{:S(2)}) %collective-permute-start) | collective-permute-done | bytes 442400 | tf_op jit(solution)/shard_map/ppermute | solution.py:257
  17.2 0.7 collective-permute-start.6
  17.9 1.5 %collective-permute-start.2 = (bf16[272,768]{1,0:T(8,128)(2,1)S(1)}, bf16[272,768]{1,0:T(8,128)(2,1)}, u32[]{:S(2)}, u32[]{:S(2)}) collective-permute-start(bf16[272,768]{1,0:T(8,128)(2,1)S(1)} %pad_maximum_fusion.refs_2_), channel_id=1, source_target_pairs={{4,8},{8,4},{5,9},{9,5},{6,10},{10,6},{7,11},{11,7},{20,24},{24,20... | collective-permute-start | bytes 1253384 | tf_op jit(solution)/shard_map/ppermute | solution.py:258
  19.3 6.1 %collective-permute-done.1.refs_3_ = bf16[272,768]{1,0:T(8,128)(2,1)} collective-permute-done((bf16[272,768]{1,0:T(8,128)(2,1)S(1)}, bf16[272,768]{1,0:T(8,128)(2,1)}, u32[]{:S(2)}, u32[]{:S(2)}) %collective-permute-start.1) | collective-permute-done | bytes 417824 | tf_op jit(solution)/shard_map/ppermute | solution.py:257
  25.4 1.4 %collective-permute-start.8 = (bf16[272,768]{1,0:T(8,128)(2,1)}, bf16[272,768]{1,0:T(8,128)(2,1)}, u32[]{:S(2)}, u32[]{:S(2)}) collective-permute-start(bf16[272,768]{1,0:T(8,128)(2,1)} %collective-permute-done.1.refs_3_), channel_id=1, source_target_pairs={{4,8},{8,4},{5,9},{9,5},{6,10},{10,6},{7,11},{11,7},{20,24},{24,20... | collective-permute-start | bytes 1253384 | tf_op jit(solution)/shard_map/ppermute | solution.py:262
  26.8 1.3 %collective-permute-start.5 = (bf16[288,768]{1,0:T(8,128)(2,1)S(1)}, bf16[288,768]{1,0:T(8,128)(2,1)S(1)}, u32[]{:S(2)}, u32[]{:S(2)}) collective-permute-start(bf16[288,768]{1,0:T(8,128)(2,1)S(1)} %collective-permute-done.4.refs_0_.refs_4_), channel_id=1, source_target_pairs={{4,0},{8,12},{5,1},{9,13},{6,2},{10,14},{7,3},{11,15},{20,16},{24,... | collective-permute-start | bytes 1327112 | tf_op jit(solution)/shard_map/ppermute | solution.py:263
  28.1 1.3 %collective-permute-start.7 = (bf16[288,768]{1,0:T(8,128)(2,1)S(1)}, bf16[288,768]{1,0:T(8,128)(2,1)S(1)}, u32[]{:S(2)}, u32[]{:S(2)}) collective-permute-start(bf16[288,768]{1,0:T(8,128)(2,1)S(1)} %collective-permute-done.6.refs_2_.refs_6_), channel_id=1, source_target_pairs={{4,0},{8,12},{5,1},{9,13},{6,2},{10,14},{7,3},{11,15},{20,16},{24,... | collective-permute-start | bytes 1327112 | tf_op jit(solution)/shard_map/ppermute | solution.py:267
  30.1 1.3 %collective-permute-start.3 = (bf16[272,768]{1,0:T(8,128)(2,1)}, bf16[272,768]{1,0:T(8,128)(2,1)}, u32[]{:S(2)}, u32[]{:S(2)}) collective-permute-start(bf16[272,768]{1,0:T(8,128)(2,1)} %collective-permute-done.2.refs_4_), channel_id=1, source_target_pairs={{4,0},{8,12},{5,1},{9,13},{6,2},{10,14},{7,3},{11,15},{20,16},{24,... | collective-permute-start | bytes 1253384 | tf_op jit(solution)/shard_map/ppermute | solution.py:263
  31.4 3.5 %pick_near0.1 = (bf16[320,768]{1,0:T(8,128)(2,1)}, bf16[320,768]{1,0:T(8,128)(2,1)}) custom-call(s32[3]{0:T(128)} %pad_add_fusion.line_ref, bf16[288,768]{1,0:T(8,128)(2,1)} %copy-done.2, bf16[288,768]{1,0:T(8,128)(2,1)} %copy-done.3, bf16[288,768]{1,0:T(8,128)(2,1)} %copy-done.2, bf16[288,768]{1,0:T(8,128)(2,1)} %copy-done.3), custom_call_target="tpu_custom_call" | custom-call | flops 100663296 | bytes 2359296 | tf_op jit(solution)/shard_map/pick_near0/pallas_call | solution.py:201
  35.0 1.3 %collective-permute-start.9 = (bf16[272,768]{1,0:T(8,128)(2,1)}, bf16[272,768]{1,0:T(8,128)(2,1)S(1)}, u32[]{:S(2)}, u32[]{:S(2)}) collective-permute-start(bf16[272,768]{1,0:T(8,128)(2,1)} %collective-permute-done.8.refs_6_), channel_id=1, source_target_pairs={{4,0},{8,12},{5,1},{9,13},{6,2},{10,14},{7,3},{11,15},{20,16},{24,... | collective-permute-start | bytes 1253384 | tf_op jit(solution)/shard_map/ppermute | solution.py:267
  36.3 1.7 %collective-permute-start.12 = (bf16[320,768]{1,0:T(8,128)(2,1)}, bf16[320,768]{1,0:T(8,128)(2,1)S(1)}, u32[]{:S(2)}, u32[]{:S(2)}) collective-permute-start(bf16[320,768]{1,0:T(8,128)(2,1)} %get-tuple-element.21), channel_id=1, source_target_pairs={{0,2},{2,0},{1,3},{3,1},{4,6},{6,4},{5,7},{7,5},{8,10},{10,8},{9,1... | collective-permute-start | bytes 1474568 | tf_op jit(solution)/shard_map/ppermute | solution.py:253
  38.0 5.0 %collective-permute-done.5.refs_1_.refs_5_ = bf16[288,768]{1,0:T(8,128)(2,1)S(1)} collective-permute-done((bf16[288,768]{1,0:T(8,128)(2,1)S(1)}, bf16[288,768]{1,0:T(8,128)(2,1)S(1)}, u32[]{:S(2)}, u32[]{:S(2)}) %collective-permute-start.5) | collective-permute-done | bytes 442400 | tf_op jit(solution)/shard_map/ppermute | solution.py:263
  43.0 9.5 %collective-permute-done.7.refs_3_.refs_7_ = bf16[288,768]{1,0:T(8,128)(2,1)S(1)} collective-permute-done((bf16[288,768]{1,0:T(8,128)(2,1)S(1)}, bf16[288,768]{1,0:T(8,128)(2,1)S(1)}, u32[]{:S(2)}, u32[]{:S(2)}) %collective-permute-start.7) | collective-permute-done | bytes 442400 | tf_op jit(solution)/shard_map/ppermute | solution.py:267
  52.5 0.8 copy-done.7
  53.3 3.8 %pick_far0.1 = (bf16[320,768]{1,0:T(8,128)(2,1)}, bf16[320,768]{1,0:T(8,128)(2,1)}) custom-call(s32[3]{0:T(128)} %pad_add_fusion.line_ref, bf16[288,768]{1,0:T(8,128)(2,1)} %copy-done.4, bf16[288,768]{1,0:T(8,128)(2,1)} %copy-done.6, bf16[288,768]{1,0:T(8,128)(2,1)} %copy-done.5, bf16[288,768]{1,0:T(8,128)(2,1)} %copy-done.7, bf16[288,768]{1,0:T(8,128)(2,1)} %copy-done.4, ...), custom_call_target="tpu_custom_call" | custom-call | flops 100663296 | bytes 2359296 | tf_op jit(solution)/shard_map/pick_far0/pallas_call | solution.py:201
  57.1 1.5 %collective-permute-start.13 = (bf16[320,768]{1,0:T(8,128)(2,1)}, bf16[320,768]{1,0:T(8,128)(2,1)S(1)}, u32[]{:S(2)}, u32[]{:S(2)}) collective-permute-start(bf16[320,768]{1,0:T(8,128)(2,1)} %get-tuple-element.22), channel_id=1, source_target_pairs={{0,2},{2,0},{1,3},{3,1},{4,6},{6,4},{5,7},{7,5},{8,10},{10,8},{9,1... | collective-permute-start | bytes 1474568 | tf_op jit(solution)/shard_map/ppermute | solution.py:253
  58.6 2.9 %collective-permute-done.3.refs_4_.refs_5_ = bf16[272,768]{1,0:T(8,128)(2,1)} collective-permute-done((bf16[272,768]{1,0:T(8,128)(2,1)}, bf16[272,768]{1,0:T(8,128)(2,1)}, u32[]{:S(2)}, u32[]{:S(2)}) %collective-permute-start.3) | collective-permute-done | bytes 417824 | tf_op jit(solution)/shard_map/ppermute | solution.py:263
  61.6 3.5 %pick_near1.1 = (bf16[288,768]{1,0:T(8,128)(2,1)}, bf16[288,768]{1,0:T(8,128)(2,1)}) custom-call(s32[3]{0:T(128)} %pad_add_fusion.line_ref, bf16[288,768]{1,0:T(8,128)(2,1)} %copy-done.2, bf16[288,768]{1,0:T(8,128)(2,1)} %copy-done.3, bf16[272,768]{1,0:T(8,128)(2,1)} %copy-done.8, bf16[272,768]{1,0:T(8,128)(2,1)} %collective-permute-done.1.refs_3_, ...), custom_call_target="tpu_custom_call" | custom-call | flops 100663296 | bytes 2359296 | tf_op jit(solution)/shard_map/pick_near1/pallas_call | solution.py:201
  65.0 1.5 %collective-permute-start.10 = (bf16[288,768]{1,0:T(8,128)(2,1)}, bf16[288,768]{1,0:T(8,128)(2,1)S(1)}, u32[]{:S(2)}, u32[]{:S(2)}) collective-permute-start(bf16[288,768]{1,0:T(8,128)(2,1)} %get-tuple-element.18), channel_id=1, source_target_pairs={{0,2},{2,0},{1,3},{3,1},{4,6},{6,4},{5,7},{7,5},{8,10},{10,8},{9,1... | collective-permute-start | bytes 1327112 | tf_op jit(solution)/shard_map/ppermute | solution.py:253
  66.5 1.8 %collective-permute-done.9.refs_7_ = bf16[272,768]{1,0:T(8,128)(2,1)S(1)} collective-permute-done((bf16[272,768]{1,0:T(8,128)(2,1)}, bf16[272,768]{1,0:T(8,128)(2,1)S(1)}, u32[]{:S(2)}, u32[]{:S(2)}) %collective-permute-start.9) | collective-permute-done | bytes 417824 | tf_op jit(solution)/shard_map/ppermute | solution.py:267
  68.3 0.8 copy-done.11
  69.1 3.7 %pick_far1.1 = (bf16[288,768]{1,0:T(8,128)(2,1)}, bf16[288,768]{1,0:T(8,128)(2,1)}) custom-call(s32[3]{0:T(128)} %pad_add_fusion.line_ref, bf16[288,768]{1,0:T(8,128)(2,1)} %copy-done.4, bf16[288,768]{1,0:T(8,128)(2,1)} %copy-done.6, bf16[288,768]{1,0:T(8,128)(2,1)} %copy-done.5, bf16[288,768]{1,0:T(8,128)(2,1)} %copy-done.7, ...), custom_call_target="tpu_custom_call" | custom-call | flops 100663296 | bytes 2359296 | tf_op jit(solution)/shard_map/pick_far1/pallas_call | solution.py:201
  72.8 1.5 %collective-permute-start.11 = (bf16[288,768]{1,0:T(8,128)(2,1)}, bf16[288,768]{1,0:T(8,128)(2,1)S(1)}, u32[]{:S(2)}, u32[]{:S(2)}) collective-permute-start(bf16[288,768]{1,0:T(8,128)(2,1)} %get-tuple-element.19), channel_id=1, source_target_pairs={{0,2},{2,0},{1,3},{3,1},{4,6},{6,4},{5,7},{7,5},{8,10},{10,8},{9,1... | collective-permute-start | bytes 1327112 | tf_op jit(solution)/shard_map/ppermute | solution.py:253
  74.4 0.8 copy-done
  75.3 12.9 %attention0.1.refs_15_ = bf16[768,1536]{1,0:T(8,128)(2,1)} custom-call(s32[3]{0:T(128)} %pad_add_fusion.line_ref, bf16[768,1536]{1,0:T(8,128)(2,1)} %refs_0_.3, bf16[768,1536]{1,0:T(8,128)(2,1)} %refs_1_.3, bf16[768,1536]{1,0:T(8,128)(2,1)} %refs_2_.3, bf16[320,768]{1,0:T(8,128)(2,1)} %get-tuple-element.15.refs_3_.refs_7_.refs_8_, ...), custom_call_target="tpu_custom_call" | custom-call | flops 589824 | bytes 1179648 | tf_op jit(solution)/shard_map/attention0/pallas_call | solution.py:128
  88.2 0.8 copy-done.9
  89.1 12.8 %attention6.1 = bf16[768,1536]{1,0:T(8,128)(2,1)} custom-call(s32[3]{0:T(128)} %pad_add_fusion.line_ref, bf16[768,1536]{1,0:T(8,128)(2,1)} %refs_0_.3, bf16[768,1536]{1,0:T(8,128)(2,1)} %refs_1_.3, bf16[768,1536]{1,0:T(8,128)(2,1)} %refs_2_.3, bf16[288,768]{1,0:T(8,128)(2,1)} %get-tuple-element.14.refs_3_, ...), custom_call_target="tpu_custom_call", output_to_operand_aliasing={{}: (16, {})} | custom-call | flops 589824 | bytes 1179648 | tf_op jit(solution)/shard_map/attention6/pallas_call | solution.py:128
  (36 shorter events, 1.4 us)
Async XLA Ops:
  3.1 28.3 %copy-start.2 = (bf16[288,768]{1,0:T(8,128)(2,1)}, bf16[288,768]{1,0:T(8,128)(2,1)S(1)}, u32[]{:S(2)}) copy-start(bf16[288,768]{1,0:T(8,128)(2,1)S(1)} %fusion.1.refs_0_.refs_2_) | copy-start | bytes 1327108
  3.1 14.1 %collective-permute-start = (bf16[288,768]{1,0:T(8,128)(2,1)S(1)}, bf16[288,768]{1,0:T(8,128)(2,1)S(1)}, u32[]{:S(2)}, u32[]{:S(2)}) collective-permute-start(bf16[288,768]{1,0:T(8,128)(2,1)S(1)} %fusion.1.refs_0_.refs_2_), channel_id=1, source_target_pairs={{0,4},{4,0},{8,12},{12,8},{1,5},{5,1},{9,13},{13,9},{2,6},{6,2},{1... | collective-permute-start | bytes 1327112 | tf_op jit(solution)/shard_map/ppermute | solution.py:257
  6.2 55.3 %copy-start.8 = (bf16[272,768]{1,0:T(8,128)(2,1)}, bf16[272,768]{1,0:T(8,128)(2,1)S(1)}, u32[]{:S(2)}) copy-start(bf16[272,768]{1,0:T(8,128)(2,1)S(1)} %pad_maximum_fusion.refs_2_) | copy-start | bytes 1253380
  6.2 19.2 %collective-permute-start.1 = (bf16[272,768]{1,0:T(8,128)(2,1)S(1)}, bf16[272,768]{1,0:T(8,128)(2,1)}, u32[]{:S(2)}, u32[]{:S(2)}) collective-permute-start(bf16[272,768]{1,0:T(8,128)(2,1)S(1)} %pad_maximum_fusion.refs_2_), channel_id=1, source_target_pairs={{0,4},{4,0},{8,12},{12,8},{1,5},{5,1},{9,13},{13,9},{2,6},{6,2},{1... | collective-permute-start | bytes 1253384 | tf_op jit(solution)/shard_map/ppermute | solution.py:257
  6.3 20.5 %collective-permute-start.4 = (bf16[288,768]{1,0:T(8,128)(2,1)S(1)}, bf16[288,768]{1,0:T(8,128)(2,1)S(1)}, u32[]{:S(2)}, u32[]{:S(2)}) collective-permute-start(bf16[288,768]{1,0:T(8,128)(2,1)S(1)} %fusion.1.refs_0_.refs_2_), channel_id=1, source_target_pairs={{4,8},{8,4},{5,9},{9,5},{6,10},{10,6},{7,11},{11,7},{20,24},{24,20... | collective-permute-start | bytes 1327112 | tf_op jit(solution)/shard_map/ppermute | solution.py:258
  17.2 14.2 %copy-start.3 = (bf16[288,768]{1,0:T(8,128)(2,1)}, bf16[288,768]{1,0:T(8,128)(2,1)S(1)}, u32[]{:S(2)}) copy-start(bf16[288,768]{1,0:T(8,128)(2,1)S(1)} %collective-permute-done.refs_1_.refs_3_) | copy-start | bytes 1327108
  17.2 10.9 %collective-permute-start.6 = (bf16[288,768]{1,0:T(8,128)(2,1)S(1)}, bf16[288,768]{1,0:T(8,128)(2,1)S(1)}, u32[]{:S(2)}, u32[]{:S(2)}) collective-permute-start(bf16[288,768]{1,0:T(8,128)(2,1)S(1)} %collective-permute-done.refs_1_.refs_3_), channel_id=1, source_target_pairs={{4,8},{8,4},{5,9},{9,5},{6,10},{10,6},{7,11},{11,7},{20,24},{24,20... | collective-permute-start | bytes 1327112 | tf_op jit(solution)/shard_map/ppermute | solution.py:262
  17.9 12.3 %collective-permute-start.2 = (bf16[272,768]{1,0:T(8,128)(2,1)S(1)}, bf16[272,768]{1,0:T(8,128)(2,1)}, u32[]{:S(2)}, u32[]{:S(2)}) collective-permute-start(bf16[272,768]{1,0:T(8,128)(2,1)S(1)} %pad_maximum_fusion.refs_2_), channel_id=1, source_target_pairs={{4,8},{8,4},{5,9},{9,5},{6,10},{10,6},{7,11},{11,7},{20,24},{24,20... | collective-permute-start | bytes 1253384 | tf_op jit(solution)/shard_map/ppermute | solution.py:258
  25.4 9.6 %collective-permute-start.8 = (bf16[272,768]{1,0:T(8,128)(2,1)}, bf16[272,768]{1,0:T(8,128)(2,1)}, u32[]{:S(2)}, u32[]{:S(2)}) collective-permute-start(bf16[272,768]{1,0:T(8,128)(2,1)} %collective-permute-done.1.refs_3_), channel_id=1, source_target_pairs={{4,8},{8,4},{5,9},{9,5},{6,10},{10,6},{7,11},{11,7},{20,24},{24,20... | collective-permute-start | bytes 1253384 | tf_op jit(solution)/shard_map/ppermute | solution.py:262
  26.8 25.7 %copy-start.4 = (bf16[288,768]{1,0:T(8,128)(2,1)}, bf16[288,768]{1,0:T(8,128)(2,1)S(1)}, u32[]{:S(2)}) copy-start(bf16[288,768]{1,0:T(8,128)(2,1)S(1)} %collective-permute-done.4.refs_0_.refs_4_) | copy-start | bytes 1327108
  26.8 16.2 %collective-permute-start.5 = (bf16[288,768]{1,0:T(8,128)(2,1)S(1)}, bf16[288,768]{1,0:T(8,128)(2,1)S(1)}, u32[]{:S(2)}, u32[]{:S(2)}) collective-permute-start(bf16[288,768]{1,0:T(8,128)(2,1)S(1)} %collective-permute-done.4.refs_0_.refs_4_), channel_id=1, source_target_pairs={{4,0},{8,12},{5,1},{9,13},{6,2},{10,14},{7,3},{11,15},{20,16},{24,... | collective-permute-start | bytes 1327112 | tf_op jit(solution)/shard_map/ppermute | solution.py:263
  28.1 24.4 %copy-start.5 = (bf16[288,768]{1,0:T(8,128)(2,1)}, bf16[288,768]{1,0:T(8,128)(2,1)S(1)}, u32[]{:S(2)}) copy-start(bf16[288,768]{1,0:T(8,128)(2,1)S(1)} %collective-permute-done.6.refs_2_.refs_6_) | copy-start | bytes 1327108
  28.1 24.4 %collective-permute-start.7 = (bf16[288,768]{1,0:T(8,128)(2,1)S(1)}, bf16[288,768]{1,0:T(8,128)(2,1)S(1)}, u32[]{:S(2)}, u32[]{:S(2)}) collective-permute-start(bf16[288,768]{1,0:T(8,128)(2,1)S(1)} %collective-permute-done.6.refs_2_.refs_6_), channel_id=1, source_target_pairs={{4,0},{8,12},{5,1},{9,13},{6,2},{10,14},{7,3},{11,15},{20,16},{24,... | collective-permute-start | bytes 1327112 | tf_op jit(solution)/shard_map/ppermute | solution.py:267
  30.1 31.4 %collective-permute-start.3 = (bf16[272,768]{1,0:T(8,128)(2,1)}, bf16[272,768]{1,0:T(8,128)(2,1)}, u32[]{:S(2)}, u32[]{:S(2)}) collective-permute-start(bf16[272,768]{1,0:T(8,128)(2,1)} %collective-permute-done.2.refs_4_), channel_id=1, source_target_pairs={{4,0},{8,12},{5,1},{9,13},{6,2},{10,14},{7,3},{11,15},{20,16},{24,... | collective-permute-start | bytes 1253384 | tf_op jit(solution)/shard_map/ppermute | solution.py:263
  35.0 33.4 %collective-permute-start.9 = (bf16[272,768]{1,0:T(8,128)(2,1)}, bf16[272,768]{1,0:T(8,128)(2,1)S(1)}, u32[]{:S(2)}, u32[]{:S(2)}) collective-permute-start(bf16[272,768]{1,0:T(8,128)(2,1)} %collective-permute-done.8.refs_6_), channel_id=1, source_target_pairs={{4,0},{8,12},{5,1},{9,13},{6,2},{10,14},{7,3},{11,15},{20,16},{24,... | collective-permute-start | bytes 1253384 | tf_op jit(solution)/shard_map/ppermute | solution.py:267
  36.3 38.1 %collective-permute-start.12 = (bf16[320,768]{1,0:T(8,128)(2,1)}, bf16[320,768]{1,0:T(8,128)(2,1)S(1)}, u32[]{:S(2)}, u32[]{:S(2)}) collective-permute-start(bf16[320,768]{1,0:T(8,128)(2,1)} %get-tuple-element.21), channel_id=1, source_target_pairs={{0,2},{2,0},{1,3},{3,1},{4,6},{6,4},{5,7},{7,5},{8,10},{10,8},{9,1... | collective-permute-start | bytes 1474568 | tf_op jit(solution)/shard_map/ppermute | solution.py:253
  43.0 9.5 %copy-start.6 = (bf16[288,768]{1,0:T(8,128)(2,1)}, bf16[288,768]{1,0:T(8,128)(2,1)S(1)}, u32[]{:S(2)}) copy-start(bf16[288,768]{1,0:T(8,128)(2,1)S(1)} %collective-permute-done.5.refs_1_.refs_5_) | copy-start | bytes 1327108
  52.5 0.8 copy-start.7
  57.1 17.2 %collective-permute-start.13 = (bf16[320,768]{1,0:T(8,128)(2,1)}, bf16[320,768]{1,0:T(8,128)(2,1)S(1)}, u32[]{:S(2)}, u32[]{:S(2)}) collective-permute-start(bf16[320,768]{1,0:T(8,128)(2,1)} %get-tuple-element.22), channel_id=1, source_target_pairs={{0,2},{2,0},{1,3},{3,1},{4,6},{6,4},{5,7},{7,5},{8,10},{10,8},{9,1... | collective-permute-start | bytes 1474568 | tf_op jit(solution)/shard_map/ppermute | solution.py:253
  65.0 23.1 %collective-permute-start.10 = (bf16[288,768]{1,0:T(8,128)(2,1)}, bf16[288,768]{1,0:T(8,128)(2,1)S(1)}, u32[]{:S(2)}, u32[]{:S(2)}) collective-permute-start(bf16[288,768]{1,0:T(8,128)(2,1)} %get-tuple-element.18), channel_id=1, source_target_pairs={{0,2},{2,0},{1,3},{3,1},{4,6},{6,4},{5,7},{7,5},{8,10},{10,8},{9,1... | collective-permute-start | bytes 1327112 | tf_op jit(solution)/shard_map/ppermute | solution.py:253
  68.3 0.8 copy-start.11
  72.8 15.3 %collective-permute-start.11 = (bf16[288,768]{1,0:T(8,128)(2,1)}, bf16[288,768]{1,0:T(8,128)(2,1)S(1)}, u32[]{:S(2)}, u32[]{:S(2)}) collective-permute-start(bf16[288,768]{1,0:T(8,128)(2,1)} %get-tuple-element.19), channel_id=1, source_target_pairs={{0,2},{2,0},{1,3},{3,1},{4,6},{6,4},{5,7},{7,5},{8,10},{10,8},{9,1... | collective-permute-start | bytes 1327112 | tf_op jit(solution)/shard_map/ppermute | solution.py:253
  74.3 0.8 copy-start
  74.4 0.9 copy-start.1
  88.2 0.8 copy-start.9
  88.2 0.9 copy-start.10

commit v3 on v2

--- a/solution.py
+++ b/solution.py
@@ -32,16 +32,68 @@
     return jnp.sum(chosen.reshape(tile_count * slot_count, window_blocks, readers), axis=2)
 
 
+def tile_kernel(q_ref, k_ref, v_ref, sum_ref, stat_ref, value_rows):
+    tok_rows = k_ref.shape[0]
+    scale = LOG2E / math.sqrt(HD)
+
+    @pl.when(pl.program_id(0) == 0)
+    def _():
+        for sub in range(STEP_HEADS):
+            value_rows[sub, :, HD:] = jnp.ones((tok_rows, HD), BF)
+        stat_ref[...] = jnp.zeros(stat_ref.shape, F32)
+
+    lane = lax.broadcasted_iota(jnp.int32, (TILE_Q, HD), 1)
+    for sub in range(STEP_HEADS):
+        head = pl.program_id(0) * STEP_HEADS + sub
+        cols = slice(sub * HD, (sub + 1) * HD)
+        value_rows[sub, :, 0:HD] = v_ref[:, cols]
+        for start in range(0, tok_rows, TILE_Q):
+            rows = slice(start, start + TILE_Q)
+            scores = lax.dot_general(
+                q_ref[rows, cols], k_ref[:, cols], (((1,), (1,)), ((), ())), preferred_element_type=F32
+            )
+            top = jnp.max(scores, axis=1, keepdims=True)
+            weights = jnp.exp2((scores - top) * scale).astype(BF)
+            mixed = jnp.dot(weights, value_rows[sub], preferred_element_type=F32)
+            sum_ref[rows, cols] = mixed[:, :HD]
+            kept = jnp.where(lane == head, top, stat_ref[rows, :])
+            stat_ref[rows, :] = jnp.where(lane == head + HD // 2, mixed[:, HD:], kept)
+
+
+def tile_attention(first, heads, queries, keys, values):
+    tok_rows, width = queries.shape
+    spec = pl.BlockSpec((tok_rows, STEP_HEADS * HD), lambda h: (0, first // STEP_HEADS + h))
+    own_spec = pl.BlockSpec((tok_rows, STEP_HEADS * HD), lambda h: (0, h))
+    return pl.pallas_call(
+        tile_kernel,
+        grid=(heads // STEP_HEADS,),
+        in_specs=[spec] * 3,
+        out_specs=(own_spec, pl.BlockSpec((tok_rows, HD), lambda h: (0, 0))),
+        out_shape=(
+            jax.ShapeDtypeStruct((tok_rows, heads * HD), F32),
+            jax.ShapeDtypeStruct((tok_rows, HD), F32),
+        ),
+        scratch_shapes=[pltpu.VMEM((STEP_HEADS, tok_rows, 2 * HD), BF)],
+        compiler_params=pltpu.CompilerParams(vmem_limit_bytes=VMEM_BYTES),
+        cost_estimate=pl.CostEstimate(
+            flops=heads * 6 * HD * tok_rows * tok_rows,
+            bytes_accessed=heads * HD * 10 * tok_rows,
+            transcendentals=heads * tok_rows * tok_rows,
+        ),
+        name="tile%d" % first,
+    )(queries, keys, values)
+
+
 def attention_kernel(settings, line_ref, *refs):
-    tok_rows, slot_rows, text_rows, parts, gathered = settings
-    q_ref, k_ref, v_ref = refs[:3]
+    slot_rows, text_rows, parts, gathered = settings
+    q_ref, k_ref, sum_ref, stat_ref = refs[:4]
     arrays = parts // 2 if gathered else parts
-    part_refs = refs[3 : 3 + arrays]
+    part_refs = refs[4 : 4 + arrays]
     if gathered:
         each = part_refs[0].shape[0] // 2
         part_refs = [part.at[half * each : (half + 1) * each, :] for part in part_refs for half in range(2)]
-    mark_refs = refs[3 + arrays : 3 + arrays + parts]
-    extra = refs[3 + arrays + parts : -4]
+    mark_refs = refs[4 + arrays : 4 + arrays + parts]
+    extra = refs[4 + arrays + parts : -4]
     out_ref, key_rows, value_rows, flag_rows = refs[-4:]
     scale = LOG2E / math.sqrt(HD)
     total = key_rows.shape[1]
@@ -59,13 +111,11 @@
                 flag_rows[rows, :] = mark[...]
         for sub in range(STEP_HEADS):
             value_rows[sub, :, HD:] = jnp.ones((total, HD), BF)
-            value_rows[sub, tok_rows : tok_rows + parts * slot_rows, HD:] = flag_rows[...]
+            value_rows[sub, 0 : parts * slot_rows, HD:] = flag_rows[...]
 
     for sub in range(STEP_HEADS):
         cols = slice(sub * HD, (sub + 1) * HD)
-        key_rows[sub, 0:tok_rows, :] = k_ref[:, cols]
-        value_rows[sub, 0:tok_rows, 0:HD] = v_ref[:, cols]
-        at = tok_rows
+        at = 0
         spare = k_ref[0:1, cols]
         for place, part in enumerate(part_refs):
             flags = flag_rows[place * slot_rows : (place + 1) * slot_rows, :]
@@ -84,24 +134,36 @@
         else:
             key_rows[sub, at:, :] = extra[0][:, cols]
             value_rows[sub, at:, 0:HD] = extra[1][:, cols]
-        for start in range(0, tok_rows, TILE_Q):
+        head = pl.program_id(0) * STEP_HEADS + sub
+        lane = lax.broadcasted_iota(jnp.int32, (TILE_Q, HD), 1)
+        for start in range(0, q_ref.shape[0], TILE_Q):
             rows = slice(start, start + TILE_Q)
             scores = lax.dot_general(
                 q_ref[rows, cols], key_rows[sub], (((1,), (1,)), ((), ())), preferred_element_type=F32
             )
-            top = jnp.max(scores, axis=1, keepdims=True)
+            stats = stat_ref[rows, :]
+            tile_top = jnp.sum(jnp.where(lane == head, stats, 0.0), axis=1, keepdims=True)
+            tile_total = jnp.sum(jnp.where(lane == head + HD // 2, stats, 0.0), axis=1, keepdims=True)
+            top = jnp.maximum(jnp.max(scores, axis=1, keepdims=True), tile_top)
             weights = jnp.exp2((scores - top) * scale).astype(BF)
             mixed = jnp.dot(weights, value_rows[sub], preferred_element_type=F32)
-            out_ref[rows, cols] = (mixed[:, :HD] / mixed[:, HD:]).astype(BF)
-
-
-def attention(first, heads, line, queries, keys, values, parts, marks, text, slot_rows, text_rows, total, out, after):
+            share = jnp.exp2((tile_top - top) * scale)
+            whole = mixed[:, :HD] + share * sum_ref[rows, cols]
+            out_ref[rows, cols] = (whole / (mixed[:, HD:] + share * tile_total)).astype(BF)
+
+
+def attention(first, heads, line, queries, keys, tile, parts, marks, text, slot_rows, text_rows, total, out, after):
     tok_rows, width = queries.shape
     wide = STEP_HEADS * HD
     col = lambda h, s: (0, first // STEP_HEADS + h)
     here = lambda h, s: (0, h)
-    specs = [pl.BlockSpec((tok_rows, wide), col)] * 3
-    operands = [line, queries, keys, values]
+    specs = [
+        pl.BlockSpec((tok_rows, wide), col),
+        pl.BlockSpec((16, wide), col),
+        pl.BlockSpec((tok_rows, wide), here),
+        pl.BlockSpec((tok_rows, HD), lambda h, s: (0, 0)),
+    ]
+    operands = [line, queries, keys, *tile]
     for part in parts:
         specs.append(pl.BlockSpec((part.shape[0], wide), col if part.shape[1] == width else here))
         operands.append(part)
@@ -124,7 +186,7 @@
     for array in after:
         specs.append(pl.BlockSpec(memory_space=pl.ANY))
         operands.append(array)
-    settings = (tok_rows, slot_rows, text_rows, len(parts) * (1 if text else 2), not text)
+    settings = (slot_rows, text_rows, len(parts) * (1 if text else 2), not text)
     return pl.pallas_call(
         functools.partial(attention_kernel, settings),
         grid_spec=pltpu.PrefetchScalarGridSpec(
@@ -135,7 +197,7 @@
             scratch_shapes=[
                 pltpu.VMEM((STEP_HEADS, total, HD), BF),
                 pltpu.VMEM((STEP_HEADS, total, 2 * HD), BF),
-                pltpu.VMEM((settings[3] * slot_rows, HD), BF),
+                pltpu.VMEM((settings[2] * slot_rows, HD), BF),
             ],
         ),
         out_shape=jax.ShapeDtypeStruct((tok_rows, width), BF),
@@ -248,6 +310,9 @@
         rows = [keys[:span, cols], values[:span, cols], words[:, cols]]
         bundles.append(jnp.concatenate(rows + [slab] if column == 0 else rows, axis=0))
         column += heads * HD
+    tiles = []
+    for heads in HEAD_CUTS:
+        tiles.append(tile_attention(len(tiles) * heads, heads, queries, keys, values))
     def take(label, sources, slabs, after):
         kept, sent = pick(label, slot_rows, span, line, sources, slabs, after)
         return kept, lax.ppermute(sent, "tm", swap)
@@ -259,6 +324,7 @@
         if g == 0:
             slabs = ((own,), (pair,))
             near.append(take("near0", slabs, slabs, ()))
+        pair, _ = lax.optimization_barrier((pair, tiles[g][1]))
         pb = lax.ppermute(pair, "space", inner)
         qa = lax.ppermute(pa, "space", outward)
         if g > 0:
@@ -270,13 +336,13 @@
     far = [take("far%d" % g, held[g], held[0], ()) for g in range(count)]
     out = None
     first = 0
-    total = tok_rows + tile_count * slot_rows + spaces * text
+    total = tile_count * slot_rows + spaces * text
     marks = [near[0][0], far[0][0], near[0][1], far[0][1]]
     for g, heads in enumerate(HEAD_CUTS):
         parts = [near[g][0], far[g][0], near[g][1], far[g][1]]
         after = (far[-1][0],) if g == 0 else ()
         out = attention(
-            first, heads, line, queries, keys, values, parts, marks, (), slot_rows, text, total, out, after
+            first, heads, line, queries, keys, tiles[g], parts, marks, (), slot_rows, text, total, out, after
         )
         first += heads
     return out
@@ -308,10 +374,11 @@
     text_k = lax.all_gather(text_keys, "space", axis=0, tiled=True)
     text_v = lax.all_gather(text_values, "space", axis=0, tiled=True)
     rows = live.shape[0]
-    total = tok_rows + rows + text_k.shape[0]
+    total = rows + text_k.shape[0]
     line = lax.axis_index("tm").reshape(1).astype(jnp.int32)
+    tile = tile_attention(0, width // HD, queries, keys, values)
     return attention(
-        0, width // HD, line, queries, keys, values, [received], [live], (text_k, text_v), rows, 0, total, None, ()
+        0, width // HD, line, queries, keys, tile, [received], [live], (text_k, text_v), rows, 0, total, None, ()
     )
 
 

time: 102 us -> 102 us (level)
  waiting for transfers between devices: 35.5 us -> 20.4 us
  Pallas kernels: 40.3 us -> 51.4 us
  starting transfers between devices: 18.8 us -> 22.3 us
    ppermute x2, waiting for transfers between devices: 16.3 us -> 0.01 us  [chained(): pair = lax.ppermute(own, 'space', ends)]
    pallas_call x0 -> x2, Pallas kernels: none -> 16.2 us  [tile_attention(): pl.pallas_call(tile_kernel, grid=(heads // STEP_HEADS,), in_specs=[spec]...]
    pallas_call x2, Pallas kernels: 25.7 us -> 20.5 us  [attention(): pl.pallas_call(functools.partial(attention_kernel, settings), grid_spec=p...]
    ppermute x2, starting transfers between devices: 3.17 us -> 7.53 us  [chained(): pair = lax.ppermute(own, 'space', ends)]
    ppermute x2, waiting for transfers between devices: 7.97 us -> 9.18 us  [chained(): qa = lax.ppermute(pa, 'space', outward)]
    unnamed x24 -> x28, local copies, waits for them, and re-layouts: 3.37 us -> 3.36 us
  transfers between devices with their start and end apart: 14 -> 14, of which waited for: 6 -> 5; matrix products, arithmetic and copies ran while one was open for 1% -> 1% of each run, Pallas kernels for 27% -> 41%
where the time goes in v3:
time: 102 us; the launch traced here: 101 us
  Pallas kernels  51.4 us (50%)
  starting transfers between devices  22.3 us (22%)
  waiting for transfers between devices  20.4 us (20%)
  local copies, waits for them, and re-layouts  4.9 us (5%)
  other arithmetic  2.16 us (2%)
    pallas_call x2, Pallas kernels, attention(): pl.pallas_call(functools.partial(attention_kernel, settings), grid_spec=p...  20.5 us
    pallas_call x2, Pallas kernels, tile_attention(): pl.pallas_call(tile_kernel, grid=(heads // STEP_HEADS,), in_specs=[spec]...  16.2 us
    pallas_call x4, Pallas kernels, pick(): pl.pallas_call(functools.partial(pick_kernel, slot_rows, span, counts), g...  14.7 us
    ppermute x2, waiting for transfers between devices, chained(): qb = lax.ppermute(beyond, 'space', outward)  10.7 us
    ppermute x2, waiting for transfers between devices, chained(): qa = lax.ppermute(pa, 'space', outward)  9.18 us
    ppermute x2, starting transfers between devices, chained(): pair = lax.ppermute(own, 'space', ends)  7.53 us
    ppermute x4, starting transfers between devices, take(): return (kept, lax.ppermute(sent, 'tm', swap))  6.11 us
    unnamed x28, local copies, waits for them, and re-layouts  3.36 us
  transfers between devices with their start and end apart: 14, of which 5 were waited for; matrix products, arithmetic and copies ran while one was open for 1% of the time, Pallas kernels for 41%

profile of v3, /device:TPU:0, one launch (start us, length us, event | category | flops | bytes accessed | tf_op | source)
XLA Modules:
  0.0 101.4 jit_solution(16534229961837252445)
XLA Ops:
  0.0 0.7 convert_bitcast_fusion
  0.9 0.8 broadcast_select_fusion
  1.8 1.3 %fusion.2 = (bf16[128,768]{1,0:T(8,128)(2,1)S(1)}, bf16[128,768]{1,0:T(8,128)(2,1)S(1)}, bf16[128,768]{1,0:T(8,128)(2,1)S(1)}, bf16[128,768]{1,0:T(8,128)(2,1)S(1)}) fusion(bf16[768,1536]{1,0:T(8,128)(2,1)} %refs_1_.3, bf16[768,1536]{1,0:T(8,128)(2,1)} %v_ref.3), kind=kLoop, calls=%fused_computation.7 | loop fusion | bytes 1572864 | tf_op jit(solution)/shard_map/slice | solution.py:310
  3.1 3.1 %collective-permute-start = (bf16[288,768]{1,0:T(8,128)(2,1)S(1)}, bf16[288,768]{1,0:T(8,128)(2,1)S(1)}, u32[]{:S(2)}, u32[]{:S(2)}) collective-permute-start(bf16[288,768]{1,0:T(8,128)(2,1)S(1)} %fusion.1.refs_0_.refs_2_), channel_id=1, source_target_pairs={{0,4},{4,0},{8,12},{12,8},{1,5},{5,1},{9,13},{13,9},{2,6},{6,2},{1... | collective-permute-start | bytes 1327112 | tf_op jit(solution)/shard_map/ppermute | solution.py:322
  6.2 0.7 collective-permute-start.2
  6.9 4.4 %collective-permute-start.1 = (bf16[272,768]{1,0:T(8,128)(2,1)S(1)}, bf16[272,768]{1,0:T(8,128)(2,1)S(1)}, u32[]{:S(2)}, u32[]{:S(2)}) collective-permute-start(bf16[272,768]{1,0:T(8,128)(2,1)S(1)} %pad_maximum_fusion.refs_2_), channel_id=1, source_target_pairs={{0,4},{4,0},{8,12},{12,8},{1,5},{5,1},{9,13},{13,9},{2,6},{6,2},{1... | collective-permute-start | bytes 1253384 | tf_op jit(solution)/shard_map/ppermute | solution.py:322
  11.4 0.7 collective-permute-start.4
  12.0 8.1 %tile0.1 = (f32[768,768]{1,0:T(8,128)}, f32[768,128]{1,0:T(8,128)}) custom-call(bf16[768,1536]{1,0:T(8,128)(2,1)} %refs_0_.3, bf16[768,1536]{1,0:T(8,128)(2,1)} %refs_1_.3, bf16[768,1536]{1,0:T(8,128)(2,1)} %v_ref.3), custom_call_target="tpu_custom_call" | custom-call | flops 2717908992 | bytes 5898240 | tf_op jit(solution)/shard_map/tile0/pallas_call | solution.py:67
  20.2 0.7 collective-permute-start.6
  20.9 8.1 %tile6.1 = (f32[768,768]{1,0:T(8,128)}, f32[768,128]{1,0:T(8,128)}) custom-call(bf16[768,1536]{1,0:T(8,128)(2,1)} %refs_0_.3, bf16[768,1536]{1,0:T(8,128)(2,1)} %refs_1_.3, bf16[768,1536]{1,0:T(8,128)(2,1)} %v_ref.3), custom_call_target="tpu_custom_call" | custom-call | flops 2717908992 | bytes 5898240 | tf_op jit(solution)/shard_map/tile6/pallas_call | solution.py:67
  29.0 1.5 %collective-permute-start.8 = (bf16[272,768]{1,0:T(8,128)(2,1)S(1)}, bf16[272,768]{1,0:T(8,128)(2,1)}, u32[]{:S(2)}, u32[]{:S(2)}) collective-permute-start(bf16[272,768]{1,0:T(8,128)(2,1)S(1)} %collective-permute-done.1.refs_3_), channel_id=1, source_target_pairs={{4,8},{8,4},{5,9},{9,5},{6,10},{10,6},{7,11},{11,7},{20,24},{24,20... | collective-permute-start | bytes 1253384 | tf_op jit(solution)/shard_map/ppermute | solution.py:328
  30.5 1.3 %collective-permute-start.5 = (bf16[288,768]{1,0:T(8,128)(2,1)S(1)}, bf16[288,768]{1,0:T(8,128)(2,1)S(1)}, u32[]{:S(2)}, u32[]{:S(2)}) collective-permute-start(bf16[288,768]{1,0:T(8,128)(2,1)S(1)} %collective-permute-done.4.refs_0_.refs_4_), channel_id=1, source_target_pairs={{4,0},{8,12},{5,1},{9,13},{6,2},{10,14},{7,3},{11,15},{20,16},{24,... | collective-permute-start | bytes 1327112 | tf_op jit(solution)/shard_map/ppermute | solution.py:329
  31.8 1.3 %collective-permute-start.7 = (bf16[288,768]{1,0:T(8,128)(2,1)S(1)}, bf16[288,768]{1,0:T(8,128)(2,1)S(1)}, u32[]{:S(2)}, u32[]{:S(2)}) collective-permute-start(bf16[288,768]{1,0:T(8,128)(2,1)S(1)} %collective-permute-done.6.refs_2_.refs_6_), channel_id=1, source_target_pairs={{4,0},{8,12},{5,1},{9,13},{6,2},{10,14},{7,3},{11,15},{20,16},{24,... | collective-permute-start | bytes 1327112 | tf_op jit(solution)/shard_map/ppermute | solution.py:333
  33.7 1.3 %collective-permute-start.3 = (bf16[272,768]{1,0:T(8,128)(2,1)S(1)}, bf16[272,768]{1,0:T(8,128)(2,1)S(1)}, u32[]{:S(2)}, u32[]{:S(2)}) collective-permute-start(bf16[272,768]{1,0:T(8,128)(2,1)S(1)} %collective-permute-done.2.refs_4_), channel_id=1, source_target_pairs={{4,0},{8,12},{5,1},{9,13},{6,2},{10,14},{7,3},{11,15},{20,16},{24,... | collective-permute-start | bytes 1253384 | tf_op jit(solution)/shard_map/ppermute | solution.py:329
  35.0 3.5 %pick_near0.1 = (bf16[320,768]{1,0:T(8,128)(2,1)}, bf16[320,768]{1,0:T(8,128)(2,1)}) custom-call(s32[3]{0:T(128)} %pad_add_fusion.line_ref, bf16[288,768]{1,0:T(8,128)(2,1)} %copy-done.2, bf16[288,768]{1,0:T(8,128)(2,1)} %copy-done.3, bf16[288,768]{1,0:T(8,128)(2,1)} %copy-done.2, bf16[288,768]{1,0:T(8,128)(2,1)} %copy-done.3), custom_call_target="tpu_custom_call" | custom-call | flops 100663296 | bytes 2359296 | tf_op jit(solution)/shard_map/pick_near0/pallas_call | solution.py:263
  38.5 1.3 %collective-permute-start.9 = (bf16[272,768]{1,0:T(8,128)(2,1)}, bf16[272,768]{1,0:T(8,128)(2,1)}, u32[]{:S(2)}, u32[]{:S(2)}) collective-permute-start(bf16[272,768]{1,0:T(8,128)(2,1)} %collective-permute-done.8.refs_6_), channel_id=1, source_target_pairs={{4,0},{8,12},{5,1},{9,13},{6,2},{10,14},{7,3},{11,15},{20,16},{24,... | collective-permute-start | bytes 1253384 | tf_op jit(solution)/shard_map/ppermute | solution.py:333
  39.8 1.6 %collective-permute-start.12 = (bf16[320,768]{1,0:T(8,128)(2,1)}, bf16[320,768]{1,0:T(8,128)(2,1)S(1)}, u32[]{:S(2)}, u32[]{:S(2)}) collective-permute-start(bf16[320,768]{1,0:T(8,128)(2,1)} %get-tuple-element.32), channel_id=1, source_target_pairs={{0,2},{2,0},{1,3},{3,1},{4,6},{6,4},{5,7},{7,5},{8,10},{10,8},{9,1... | collective-permute-start | bytes 1474568 | tf_op jit(solution)/shard_map/ppermute | solution.py:318
  41.4 6.4 %collective-permute-done.5.refs_1_.refs_5_ = bf16[288,768]{1,0:T(8,128)(2,1)S(1)} collective-permute-done((bf16[288,768]{1,0:T(8,128)(2,1)S(1)}, bf16[288,768]{1,0:T(8,128)(2,1)S(1)}, u32[]{:S(2)}, u32[]{:S(2)}) %collective-permute-start.5) | collective-permute-done | bytes 442400 | tf_op jit(solution)/shard_map/ppermute | solution.py:329
  47.8 9.5 %collective-permute-done.7.refs_3_.refs_7_ = bf16[288,768]{1,0:T(8,128)(2,1)S(1)} collective-permute-done((bf16[288,768]{1,0:T(8,128)(2,1)S(1)}, bf16[288,768]{1,0:T(8,128)(2,1)S(1)}, u32[]{:S(2)}, u32[]{:S(2)}) %collective-permute-start.7) | collective-permute-done | bytes 442400 | tf_op jit(solution)/shard_map/ppermute | solution.py:333
  57.3 0.8 copy-done.7
  58.1 3.9 %pick_far0.1 = (bf16[320,768]{1,0:T(8,128)(2,1)}, bf16[320,768]{1,0:T(8,128)(2,1)}) custom-call(s32[3]{0:T(128)} %pad_add_fusion.line_ref, bf16[288,768]{1,0:T(8,128)(2,1)} %copy-done.4, bf16[288,768]{1,0:T(8,128)(2,1)} %copy-done.6, bf16[288,768]{1,0:T(8,128)(2,1)} %copy-done.5, bf16[288,768]{1,0:T(8,128)(2,1)} %copy-done.7, bf16[288,768]{1,0:T(8,128)(2,1)} %copy-done.4, ...), custom_call_target="tpu_custom_call" | custom-call | flops 100663296 | bytes 2359296 | tf_op jit(solution)/shard_map/pick_far0/pallas_call | solution.py:263
  61.9 1.6 %collective-permute-start.13 = (bf16[320,768]{1,0:T(8,128)(2,1)}, bf16[320,768]{1,0:T(8,128)(2,1)S(1)}, u32[]{:S(2)}, u32[]{:S(2)}) collective-permute-start(bf16[320,768]{1,0:T(8,128)(2,1)} %get-tuple-element.33), channel_id=1, source_target_pairs={{0,2},{2,0},{1,3},{3,1},{4,6},{6,4},{5,7},{7,5},{8,10},{10,8},{9,1... | collective-permute-start | bytes 1474568 | tf_op jit(solution)/shard_map/ppermute | solution.py:318
  63.5 2.8 %collective-permute-done.3.refs_4_.refs_5_ = bf16[272,768]{1,0:T(8,128)(2,1)S(1)} collective-permute-done((bf16[272,768]{1,0:T(8,128)(2,1)S(1)}, bf16[272,768]{1,0:T(8,128)(2,1)S(1)}, u32[]{:S(2)}, u32[]{:S(2)}) %collective-permute-start.3) | collective-permute-done | bytes 417824 | tf_op jit(solution)/shard_map/ppermute | solution.py:329
  66.3 0.8 copy-done.9
  67.0 3.5 %pick_near1.1 = (bf16[288,768]{1,0:T(8,128)(2,1)}, bf16[288,768]{1,0:T(8,128)(2,1)}) custom-call(s32[3]{0:T(128)} %pad_add_fusion.line_ref, bf16[288,768]{1,0:T(8,128)(2,1)} %copy-done.2, bf16[288,768]{1,0:T(8,128)(2,1)} %copy-done.3, bf16[272,768]{1,0:T(8,128)(2,1)} %copy-done.8, bf16[272,768]{1,0:T(8,128)(2,1)} %copy-done.13, bf16[272,768]{1,0:T(8,128)(2,1)} %copy-done.9), custom_call_target="tpu_custom_call" | custom-call | flops 100663296 | bytes 2359296 | tf_op jit(solution)/shard_map/pick_near1/pallas_call | solution.py:263
  70.5 1.5 %collective-permute-start.10 = (bf16[288,768]{1,0:T(8,128)(2,1)}, bf16[288,768]{1,0:T(8,128)(2,1)S(1)}, u32[]{:S(2)}, u32[]{:S(2)}) collective-permute-start(bf16[288,768]{1,0:T(8,128)(2,1)} %get-tuple-element.29), channel_id=1, source_target_pairs={{0,2},{2,0},{1,3},{3,1},{4,6},{6,4},{5,7},{7,5},{8,10},{10,8},{9,1... | collective-permute-start | bytes 1327112 | tf_op jit(solution)/shard_map/ppermute | solution.py:318
  72.0 1.2 %collective-permute-done.9.refs_7_ = bf16[272,768]{1,0:T(8,128)(2,1)} collective-permute-done((bf16[272,768]{1,0:T(8,128)(2,1)}, bf16[272,768]{1,0:T(8,128)(2,1)}, u32[]{:S(2)}, u32[]{:S(2)}) %collective-permute-start.9) | collective-permute-done | bytes 417824 | tf_op jit(solution)/shard_map/ppermute | solution.py:333
  73.3 3.8 %pick_far1.1 = (bf16[288,768]{1,0:T(8,128)(2,1)}, bf16[288,768]{1,0:T(8,128)(2,1)}) custom-call(s32[3]{0:T(128)} %pad_add_fusion.line_ref, bf16[288,768]{1,0:T(8,128)(2,1)} %copy-done.4, bf16[288,768]{1,0:T(8,128)(2,1)} %copy-done.6, bf16[288,768]{1,0:T(8,128)(2,1)} %copy-done.5, bf16[288,768]{1,0:T(8,128)(2,1)} %copy-done.7, bf16[272,768]{1,0:T(8,128)(2,1)} %copy-done.12, ...), custom_call_target="tpu_custom_call" | custom-call | flops 100663296 | bytes 2359296 | tf_op jit(solution)/shard_map/pick_far1/pallas_call | solution.py:263
  77.0 1.5 %collective-permute-start.11 = (bf16[288,768]{1,0:T(8,128)(2,1)}, bf16[288,768]{1,0:T(8,128)(2,1)S(1)}, u32[]{:S(2)}, u32[]{:S(2)}) collective-permute-start(bf16[288,768]{1,0:T(8,128)(2,1)} %get-tuple-element.30), channel_id=1, source_target_pairs={{0,2},{2,0},{1,3},{3,1},{4,6},{6,4},{5,7},{7,5},{8,10},{10,8},{9,1... | collective-permute-start | bytes 1327112 | tf_op jit(solution)/shard_map/ppermute | solution.py:318
  78.5 0.8 copy-done
  79.6 10.2 %attention0.1.refs_16_ = bf16[768,1536]{1,0:T(8,128)(2,1)} custom-call(s32[3]{0:T(128)} %pad_add_fusion.line_ref, bf16[768,1536]{1,0:T(8,128)(2,1)} %refs_0_.3, bf16[768,1536]{1,0:T(8,128)(2,1)} %refs_1_.3, f32[768,768]{1,0:T(8,128)} %get-tuple-element.34.refs_2_, f32[768,128]{1,0:T(8,128)} %get-tuple-element.24.refs_3_, ...), custom_call_target="tpu_custom_call" | custom-call | flops 589824 | bytes 1179648 | tf_op jit(solution)/shard_map/attention0/pallas_call | solution.py:190
  91.1 10.2 %attention6.1 = bf16[768,1536]{1,0:T(8,128)(2,1)} custom-call(s32[3]{0:T(128)} %pad_add_fusion.line_ref, bf16[768,1536]{1,0:T(8,128)(2,1)} %refs_0_.3, bf16[768,1536]{1,0:T(8,128)(2,1)} %refs_1_.3, f32[768,768]{1,0:T(8,128)} %get-tuple-element.20.refs_2_, f32[768,128]{1,0:T(8,128)} %get-tuple-element.21.refs_3_, ...), custom_call_target="tpu_custom_call", output_to_operand_aliasing={{}: (17, {})} | custom-call | flops 589824 | bytes 1179648 | tf_op jit(solution)/shard_map/attention6/pallas_call | solution.py:190
  (42 shorter events, 2.5 us)
Async XLA Ops:
  3.1 17.1 %copy-start.2 = (bf16[288,768]{1,0:T(8,128)(2,1)}, bf16[288,768]{1,0:T(8,128)(2,1)S(1)}, u32[]{:S(2)}) copy-start(bf16[288,768]{1,0:T(8,128)(2,1)S(1)} %fusion.1.refs_0_.refs_2_) | copy-start | bytes 1327108
  3.1 17.1 %collective-permute-start = (bf16[288,768]{1,0:T(8,128)(2,1)S(1)}, bf16[288,768]{1,0:T(8,128)(2,1)S(1)}, u32[]{:S(2)}, u32[]{:S(2)}) collective-permute-start(bf16[288,768]{1,0:T(8,128)(2,1)S(1)} %fusion.1.refs_0_.refs_2_), channel_id=1, source_target_pairs={{0,4},{4,0},{8,12},{12,8},{1,5},{5,1},{9,13},{13,9},{2,6},{6,2},{1... | collective-permute-start | bytes 1327112 | tf_op jit(solution)/shard_map/ppermute | solution.py:322
  6.2 13.9 %copy-start.8 = (bf16[272,768]{1,0:T(8,128)(2,1)}, bf16[272,768]{1,0:T(8,128)(2,1)S(1)}, u32[]{:S(2)}) copy-start(bf16[272,768]{1,0:T(8,128)(2,1)S(1)} %pad_maximum_fusion.refs_2_) | copy-start | bytes 1253380
  6.2 27.5 %collective-permute-start.2 = (bf16[272,768]{1,0:T(8,128)(2,1)S(1)}, bf16[272,768]{1,0:T(8,128)(2,1)S(1)}, u32[]{:S(2)}, u32[]{:S(2)}) collective-permute-start(bf16[272,768]{1,0:T(8,128)(2,1)S(1)} %pad_maximum_fusion.refs_2_), channel_id=1, source_target_pairs={{4,8},{8,4},{5,9},{9,5},{6,10},{10,6},{7,11},{11,7},{20,24},{24,20... | collective-permute-start | bytes 1253384 | tf_op jit(solution)/shard_map/ppermute | solution.py:323
  6.9 22.1 %collective-permute-start.1 = (bf16[272,768]{1,0:T(8,128)(2,1)S(1)}, bf16[272,768]{1,0:T(8,128)(2,1)S(1)}, u32[]{:S(2)}, u32[]{:S(2)}) collective-permute-start(bf16[272,768]{1,0:T(8,128)(2,1)S(1)} %pad_maximum_fusion.refs_2_), channel_id=1, source_target_pairs={{0,4},{4,0},{8,12},{12,8},{1,5},{5,1},{9,13},{13,9},{2,6},{6,2},{1... | collective-permute-start | bytes 1253384 | tf_op jit(solution)/shard_map/ppermute | solution.py:322
  11.4 19.1 %collective-permute-start.4 = (bf16[288,768]{1,0:T(8,128)(2,1)S(1)}, bf16[288,768]{1,0:T(8,128)(2,1)S(1)}, u32[]{:S(2)}, u32[]{:S(2)}) collective-permute-start(bf16[288,768]{1,0:T(8,128)(2,1)S(1)} %fusion.1.refs_0_.refs_2_), channel_id=1, source_target_pairs={{4,8},{8,4},{5,9},{9,5},{6,10},{10,6},{7,11},{11,7},{20,24},{24,20... | collective-permute-start | bytes 1327112 | tf_op jit(solution)/shard_map/ppermute | solution.py:323
  20.2 8.8 %copy-start.3 = (bf16[288,768]{1,0:T(8,128)(2,1)}, bf16[288,768]{1,0:T(8,128)(2,1)S(1)}, u32[]{:S(2)}) copy-start(bf16[288,768]{1,0:T(8,128)(2,1)S(1)} %collective-permute-done.refs_1_.refs_3_) | copy-start | bytes 1327108
  20.2 11.6 %collective-permute-start.6 = (bf16[288,768]{1,0:T(8,128)(2,1)S(1)}, bf16[288,768]{1,0:T(8,128)(2,1)S(1)}, u32[]{:S(2)}, u32[]{:S(2)}) collective-permute-start(bf16[288,768]{1,0:T(8,128)(2,1)S(1)} %collective-permute-done.refs_1_.refs_3_), channel_id=1, source_target_pairs={{4,8},{8,4},{5,9},{9,5},{6,10},{10,6},{7,11},{11,7},{20,24},{24,20... | collective-permute-start | bytes 1327112 | tf_op jit(solution)/shard_map/ppermute | solution.py:328
  29.0 32.9 %copy-start.13 = (bf16[272,768]{1,0:T(8,128)(2,1)}, bf16[272,768]{1,0:T(8,128)(2,1)S(1)}, u32[]{:S(2)}) copy-start(bf16[272,768]{1,0:T(8,128)(2,1)S(1)} %collective-permute-done.1.refs_3_) | copy-start | bytes 1253380
  29.0 9.5 %collective-permute-start.8 = (bf16[272,768]{1,0:T(8,128)(2,1)S(1)}, bf16[272,768]{1,0:T(8,128)(2,1)}, u32[]{:S(2)}, u32[]{:S(2)}) collective-permute-start(bf16[272,768]{1,0:T(8,128)(2,1)S(1)} %collective-permute-done.1.refs_3_), channel_id=1, source_target_pairs={{4,8},{8,4},{5,9},{9,5},{6,10},{10,6},{7,11},{11,7},{20,24},{24,20... | collective-permute-start | bytes 1253384 | tf_op jit(solution)/shard_map/ppermute | solution.py:328
  30.5 26.8 %copy-start.4 = (bf16[288,768]{1,0:T(8,128)(2,1)}, bf16[288,768]{1,0:T(8,128)(2,1)S(1)}, u32[]{:S(2)}) copy-start(bf16[288,768]{1,0:T(8,128)(2,1)S(1)} %collective-permute-done.4.refs_0_.refs_4_) | copy-start | bytes 1327108
  30.5 17.3 %collective-permute-start.5 = (bf16[288,768]{1,0:T(8,128)(2,1)S(1)}, bf16[288,768]{1,0:T(8,128)(2,1)S(1)}, u32[]{:S(2)}, u32[]{:S(2)}) collective-permute-start(bf16[288,768]{1,0:T(8,128)(2,1)S(1)} %collective-permute-done.4.refs_0_.refs_4_), channel_id=1, source_target_pairs={{4,0},{8,12},{5,1},{9,13},{6,2},{10,14},{7,3},{11,15},{20,16},{24,... | collective-permute-start | bytes 1327112 | tf_op jit(solution)/shard_map/ppermute | solution.py:329
  31.8 25.5 %copy-start.5 = (bf16[288,768]{1,0:T(8,128)(2,1)}, bf16[288,768]{1,0:T(8,128)(2,1)S(1)}, u32[]{:S(2)}) copy-start(bf16[288,768]{1,0:T(8,128)(2,1)S(1)} %collective-permute-done.6.refs_2_.refs_6_) | copy-start | bytes 1327108
  31.8 25.5 %collective-permute-start.7 = (bf16[288,768]{1,0:T(8,128)(2,1)S(1)}, bf16[288,768]{1,0:T(8,128)(2,1)S(1)}, u32[]{:S(2)}, u32[]{:S(2)}) collective-permute-start(bf16[288,768]{1,0:T(8,128)(2,1)S(1)} %collective-permute-done.6.refs_2_.refs_6_), channel_id=1, source_target_pairs={{4,0},{8,12},{5,1},{9,13},{6,2},{10,14},{7,3},{11,15},{20,16},{24,... | collective-permute-start | bytes 1327112 | tf_op jit(solution)/shard_map/ppermute | solution.py:333
  33.7 28.2 %copy-start.12 = (bf16[272,768]{1,0:T(8,128)(2,1)}, bf16[272,768]{1,0:T(8,128)(2,1)S(1)}, u32[]{:S(2)}) copy-start(bf16[272,768]{1,0:T(8,128)(2,1)S(1)} %collective-permute-done.2.refs_4_) | copy-start | bytes 1253380
  33.7 32.5 %collective-permute-start.3 = (bf16[272,768]{1,0:T(8,128)(2,1)S(1)}, bf16[272,768]{1,0:T(8,128)(2,1)S(1)}, u32[]{:S(2)}, u32[]{:S(2)}) collective-permute-start(bf16[272,768]{1,0:T(8,128)(2,1)S(1)} %collective-permute-done.2.refs_4_), channel_id=1, source_target_pairs={{4,0},{8,12},{5,1},{9,13},{6,2},{10,14},{7,3},{11,15},{20,16},{24,... | collective-permute-start | bytes 1253384 | tf_op jit(solution)/shard_map/ppermute | solution.py:329
  38.5 34.7 %collective-permute-start.9 = (bf16[272,768]{1,0:T(8,128)(2,1)}, bf16[272,768]{1,0:T(8,128)(2,1)}, u32[]{:S(2)}, u32[]{:S(2)}) collective-permute-start(bf16[272,768]{1,0:T(8,128)(2,1)} %collective-permute-done.8.refs_6_), channel_id=1, source_target_pairs={{4,0},{8,12},{5,1},{9,13},{6,2},{10,14},{7,3},{11,15},{20,16},{24,... | collective-permute-start | bytes 1253384 | tf_op jit(solution)/shard_map/ppermute | solution.py:333
  39.8 38.7 %collective-permute-start.12 = (bf16[320,768]{1,0:T(8,128)(2,1)}, bf16[320,768]{1,0:T(8,128)(2,1)S(1)}, u32[]{:S(2)}, u32[]{:S(2)}) collective-permute-start(bf16[320,768]{1,0:T(8,128)(2,1)} %get-tuple-element.32), channel_id=1, source_target_pairs={{0,2},{2,0},{1,3},{3,1},{4,6},{6,4},{5,7},{7,5},{8,10},{10,8},{9,1... | collective-permute-start | bytes 1474568 | tf_op jit(solution)/shard_map/ppermute | solution.py:318
  47.8 9.5 %copy-start.6 = (bf16[288,768]{1,0:T(8,128)(2,1)}, bf16[288,768]{1,0:T(8,128)(2,1)S(1)}, u32[]{:S(2)}) copy-start(bf16[288,768]{1,0:T(8,128)(2,1)S(1)} %collective-permute-done.5.refs_1_.refs_5_) | copy-start | bytes 1327108
  57.3 0.8 copy-start.7
  61.9 16.6 %collective-permute-start.13 = (bf16[320,768]{1,0:T(8,128)(2,1)}, bf16[320,768]{1,0:T(8,128)(2,1)S(1)}, u32[]{:S(2)}, u32[]{:S(2)}) collective-permute-start(bf16[320,768]{1,0:T(8,128)(2,1)} %get-tuple-element.33), channel_id=1, source_target_pairs={{0,2},{2,0},{1,3},{3,1},{4,6},{6,4},{5,7},{7,5},{8,10},{10,8},{9,1... | collective-permute-start | bytes 1474568 | tf_op jit(solution)/shard_map/ppermute | solution.py:318
  66.2 0.8 copy-start.9
  70.5 19.3 %collective-permute-start.10 = (bf16[288,768]{1,0:T(8,128)(2,1)}, bf16[288,768]{1,0:T(8,128)(2,1)S(1)}, u32[]{:S(2)}, u32[]{:S(2)}) collective-permute-start(bf16[288,768]{1,0:T(8,128)(2,1)} %get-tuple-element.29), channel_id=1, source_target_pairs={{0,2},{2,0},{1,3},{3,1},{4,6},{6,4},{5,7},{7,5},{8,10},{10,8},{9,1... | collective-permute-start | bytes 1327112 | tf_op jit(solution)/shard_map/ppermute | solution.py:318
  77.0 13.3 %collective-permute-start.11 = (bf16[288,768]{1,0:T(8,128)(2,1)}, bf16[288,768]{1,0:T(8,128)(2,1)S(1)}, u32[]{:S(2)}, u32[]{:S(2)}) collective-permute-start(bf16[288,768]{1,0:T(8,128)(2,1)} %get-tuple-element.30), channel_id=1, source_target_pairs={{0,2},{2,0},{1,3},{3,1},{4,6},{6,4},{5,7},{7,5},{8,10},{10,8},{9,1... | collective-permute-start | bytes 1327112 | tf_op jit(solution)/shard_map/ppermute | solution.py:318
  78.5 0.8 copy-start
  78.5 1.0 %copy-start.1 = (bf16[320,768]{1,0:T(8,128)(2,1)}, bf16[320,768]{1,0:T(8,128)(2,1)S(1)}, u32[]{:S(2)}) copy-start(bf16[320,768]{1,0:T(8,128)(2,1)S(1)} %collective-permute-done.13.refs_7_.refs_14_.refs_15_) | copy-start | bytes 1474564
  89.8 0.8 copy-start.10
  90.3 0.8 copy-start.11
